TPU v7x, 32 devices: a whole 2x2x4 slice. The times are simulated.
32 devices in a mesh: fsdp: 4 (over z), ctx: 4 (over y, core), tp: 2 (over x).
Axes of the slice: x: 2, y: 2, z: 4, core: 2. Of those that a mesh axis runs over, the one named last changes fastest.
Arguments:
- tokens: bfloat16 [8, 1024, 1536], P('fsdp', 'ctx'), may hold values from -6 to 6
- segments: int32 [8, 1024], P('fsdp'), may hold values from 0 to 1023, as said below
- cotangent: bfloat16 [8, 1024, 1536], P('fsdp', 'ctx'), may hold values from -6 to 6
- gain_attn: bfloat16 [1536], P(('fsdp', 'ctx')), may hold values from 0.5 to 1.5
- w_query: bfloat16 [1536, 1536], P(('fsdp', 'ctx'), 'tp'), may hold values from -0.15625 to 0.15625
- w_key: bfloat16 [1536, 768], P(('fsdp', 'ctx'), 'tp'), may hold values from -0.15625 to 0.15625
- w_value: bfloat16 [1536, 768], P(('fsdp', 'ctx'), 'tp'), may hold values from -0.15625 to 0.15625
- w_out: bfloat16 [1536, 1536], P('tp', ('fsdp', 'ctx')), may hold values from -1.75 to 1.75
- gain_mlp: bfloat16 [1536], P(('fsdp', 'ctx')), may hold values from 0.5 to 1.5
- w_gate: bfloat16 [1536, 4096], P(('fsdp', 'ctx'), 'tp'), may hold values from -0.15625 to 0.15625
- w_up: bfloat16 [1536, 4096], P(('fsdp', 'ctx'), 'tp'), may hold values from -0.15625 to 0.15625
- w_down: bfloat16 [4096, 1536], P('tp', ('fsdp', 'ctx')), may hold values from -0.09375 to 0.09375
Outputs:
- output: bfloat16 [8, 1024, 1536], P('fsdp', 'ctx')
- grad_tokens: float32 [8, 1024, 1536], P('fsdp', 'ctx')
- grad_gain_attn: float32 [1536], P(('fsdp', 'ctx'))
- grad_query: float32 [1536, 1536], P(('fsdp', 'ctx'), 'tp')
- grad_key: float32 [1536, 768], P(('fsdp', 'ctx'), 'tp')
- grad_value: float32 [1536, 768], P(('fsdp', 'ctx'), 'tp')
- grad_out: float32 [1536, 1536], P('tp', ('fsdp', 'ctx'))
- grad_gain_mlp: float32 [1536], P(('fsdp', 'ctx'))
- grad_gate: float32 [1536, 4096], P(('fsdp', 'ctx'), 'tp')
- grad_up: float32 [1536, 4096], P(('fsdp', 'ctx'), 'tp')
- grad_down: float32 [4096, 1536], P('tp', ('fsdp', 'ctx'))
Inputs may be any that keep to these rules, and one draw needn't show every extreme that they name: `segments`: segment numbers start at 0 in each sequence and never fall; the last position of every sequence carries 1024 - 1; in every sequence one document covers positions 255 through 1024 - 256.
All inputs are finite; a program needn't handle non-finite values.
Results may differ from a plain program's by a relative error of at most 0.018.
Values may be sent and summed in bfloat16 or wider, within the bound.
A program may use at most 192 MiB of HBM per device.

v0:
```python
import math

import jax
import jax.numpy as jnp
from jax import lax
from jax.sharding import PartitionSpec as P

HD = 96
GROUP = 2


epsilon = 1e-05
rope_base = 100000.0
negative = -1e30


def rope_tables(positions):
    half_width = HD // 2
    frequency = rope_base ** (-(2.0 * jnp.arange(half_width, dtype=jnp.float32)) / HD)
    angles = positions.astype(jnp.float32)[:, None] * frequency[None, :]
    return (jnp.cos(angles), jnp.sin(angles))


def rotate(vectors, cosine_table, sine_table):
    half_width = vectors.shape[-1] // 2
    former = vectors[..., :half_width]
    latter = vectors[..., half_width:]
    return jnp.concatenate(
        [former * cosine_table - latter * sine_table, latter * cosine_table + former * sine_table],
        axis=-1,
    )


def head_sum(partial_rows):
    return lax.psum(partial_rows.astype(jnp.bfloat16), "tp").astype(jnp.float32)


def weight_gather(shards):
    row_parts = (
        lax.all_gather(shards[0], ("fsdp", "ctx"), axis=0, tiled=True),
        lax.all_gather(shards[1], ("fsdp", "ctx"), axis=0, tiled=True),
        lax.all_gather(shards[2], ("fsdp", "ctx"), axis=0, tiled=True),
        lax.all_gather(shards[3], ("fsdp", "ctx"), axis=0, tiled=True),
        lax.all_gather(shards[4], ("fsdp", "ctx"), axis=0, tiled=True),
        lax.all_gather(shards[5], ("fsdp", "ctx"), axis=0, tiled=True),
        lax.all_gather(shards[6], ("fsdp", "ctx"), axis=0, tiled=True),
    )
    column_parts = (
        lax.all_gather(shards[7], ("fsdp", "ctx"), axis=1, tiled=True),
        lax.all_gather(shards[8], ("fsdp", "ctx"), axis=1, tiled=True),
    )
    return tuple(row_parts) + tuple(column_parts)


def grad_reduce(gradients):
    row_parts = (
        lax.psum_scatter(gradients[0], ("fsdp", "ctx"), scatter_dimension=0, tiled=True),
        lax.psum_scatter(gradients[1], ("fsdp", "ctx"), scatter_dimension=0, tiled=True),
        lax.psum_scatter(gradients[2], ("fsdp", "ctx"), scatter_dimension=0, tiled=True),
        lax.psum_scatter(gradients[3], ("fsdp", "ctx"), scatter_dimension=0, tiled=True),
        lax.psum_scatter(gradients[4], ("fsdp", "ctx"), scatter_dimension=0, tiled=True),
        lax.psum_scatter(gradients[5], ("fsdp", "ctx"), scatter_dimension=0, tiled=True),
        lax.psum_scatter(gradients[6], ("fsdp", "ctx"), scatter_dimension=0, tiled=True),
    )
    column_parts = (
        lax.psum_scatter(gradients[7], ("fsdp", "ctx"), scatter_dimension=1, tiled=True),
        lax.psum_scatter(gradients[8], ("fsdp", "ctx"), scatter_dimension=1, tiled=True),
    )
    return tuple(row_parts) + tuple(column_parts)


def block_scores(queries, key_block, query_seg, positions, key_seg, key_start):
    score_scale = 1.0 / math.sqrt(queries.shape[-1])
    key_positions = key_start + jnp.arange(key_block.shape[0], dtype=jnp.int32)
    allowed = (query_seg[:, None] == key_seg[None, :]) & (
        positions[:, None] >= key_positions[None, :]
    )
    raw_scores = jnp.einsum(
        "qhgd,khd->hgqk", queries, key_block, preferred_element_type=jnp.float32
    )
    return (jnp.where(allowed, raw_scores * score_scale, negative), allowed)


def block_fetch(
    key_all, value_all, segment_row, block_index, block_keys, last_position, first_segment
):
    key_start = block_index * block_keys
    key_block = lax.dynamic_slice_in_dim(key_all, key_start, block_keys, 0)
    value_block = lax.dynamic_slice_in_dim(value_all, key_start, block_keys, 0)
    key_seg = lax.dynamic_slice_in_dim(segment_row, key_start, block_keys, 0)
    needed = (key_start <= last_position) & (key_seg[block_keys - 1] >= first_segment)
    return (key_start, key_block, value_block, key_seg, needed)


def attention_forward(queries, key_all, value_all, segment_row, query_seg, positions):
    row_count, heads_kv, group_size, head_dim = queries.shape
    length = key_all.shape[0]
    block_keys = math.gcd(512, length)
    block_total = length // block_keys
    last_position = positions[row_count - 1]
    first_segment = query_seg[0]

    def stats_step(block_index, state):
        key_start, key_block, value_block, key_seg, needed = block_fetch(
            key_all, value_all, segment_row, block_index, block_keys, last_position, first_segment
        )
        top_old, total_old = state
        scores, allowed = block_scores(queries, key_block, query_seg, positions, key_seg, key_start)
        top_new = jnp.maximum(top_old, jnp.max(scores, axis=-1))
        weights = jnp.where(allowed, jnp.exp(scores - top_new[..., None]), 0.0)
        return (top_new, total_old * jnp.exp(top_old - top_new) + jnp.sum(weights, axis=-1))

    start_top = jnp.full((heads_kv, group_size, row_count), negative, jnp.float32)
    row_top, row_total = lax.fori_loop(
        0, block_total, stats_step, (start_top, jnp.zeros_like(start_top))
    )

    def output_step(block_index, state):
        key_start, key_block, value_block, key_seg, needed = block_fetch(
            key_all, value_all, segment_row, block_index, block_keys, last_position, first_segment
        )
        scores, allowed = block_scores(queries, key_block, query_seg, positions, key_seg, key_start)
        probability = (
            jnp.where(allowed, jnp.exp(scores - row_top[..., None]), 0.0) / row_total[..., None]
        )
        return state + jnp.einsum(
            "hgqk,khd->qhgd",
            probability.astype(jnp.bfloat16),
            value_block,
            preferred_element_type=jnp.float32,
        )

    start_out = jnp.zeros((row_count, heads_kv, group_size, head_dim), jnp.float32)
    out_low = lax.fori_loop(0, block_total, output_step, start_out)
    return (row_top, row_total, out_low)


def attention_backward(
    queries,
    key_all,
    value_all,
    segment_row,
    query_seg,
    positions,
    row_top,
    row_total,
    grad_mixed,
    row_delta,
):
    row_count, heads_kv, group_size, head_dim = queries.shape
    length = key_all.shape[0]
    block_keys = math.gcd(512, length)
    block_total = length // block_keys
    last_position = positions[row_count - 1]
    first_segment = query_seg[0]
    score_scale = 1.0 / math.sqrt(head_dim)

    def grad_step(block_index, state):
        key_start, key_block, value_block, key_seg, needed = block_fetch(
            key_all, value_all, segment_row, block_index, block_keys, last_position, first_segment
        )
        grad_query, grad_keys, grad_values = state
        scores, allowed = block_scores(queries, key_block, query_seg, positions, key_seg, key_start)
        probability = (
            jnp.where(allowed, jnp.exp(scores - row_top[..., None]), 0.0) / row_total[..., None]
        )
        grad_prob = jnp.einsum(
            "qhgd,khd->hgqk", grad_mixed, value_block, preferred_element_type=jnp.float32
        )
        grad_score = (probability * (grad_prob - row_delta[..., None]) * score_scale).astype(
            jnp.bfloat16
        )
        grad_query = grad_query + jnp.einsum(
            "hgqk,khd->qhgd", grad_score, key_block, preferred_element_type=jnp.float32
        )
        key_part = jnp.einsum(
            "hgqk,qhgd->khd", grad_score, queries, preferred_element_type=jnp.float32
        )
        value_part = jnp.einsum(
            "hgqk,qhgd->khd",
            probability.astype(jnp.bfloat16),
            grad_mixed,
            preferred_element_type=jnp.float32,
        )
        grad_keys = lax.dynamic_update_slice_in_dim(grad_keys, key_part, key_start, 0)
        grad_values = lax.dynamic_update_slice_in_dim(grad_values, value_part, key_start, 0)
        return (grad_query, grad_keys, grad_values)

    start_query = jnp.zeros((row_count, heads_kv, group_size, head_dim), jnp.float32)
    start_keys = jnp.zeros((length, heads_kv, head_dim), jnp.float32)
    return lax.fori_loop(0, block_total, grad_step, (start_query, start_keys, start_keys))


def micro_step(gathered, token_rows, segment_row, grad_in, positions, cosine_table, sine_table):
    gain_attn, w_query, w_key, w_value, gain_mlp, w_gate, w_up, w_out, w_down = gathered
    row_count = token_rows.shape[0]
    heads_kv = w_key.shape[1] // HD
    cos_four = cosine_table[:, None, None, :]
    sin_four = sine_table[:, None, None, :]
    cos_three = cosine_table[:, None, :]
    sin_three = sine_table[:, None, :]
    query_seg = lax.dynamic_slice_in_dim(segment_row, positions[0], row_count, 0)
    gain_first = gain_attn.astype(jnp.float32)
    gain_second = gain_mlp.astype(jnp.float32)
    inputs = token_rows.astype(jnp.float32)
    scale_first = lax.rsqrt(jnp.mean(inputs * inputs, axis=-1, keepdims=True) + epsilon)
    normal_first = inputs * scale_first
    normed = (normal_first * gain_first).astype(jnp.bfloat16)
    query_raw = jnp.dot(normed, w_query, preferred_element_type=jnp.float32).reshape(
        row_count, heads_kv, GROUP, HD
    )
    key_raw = jnp.dot(normed, w_key, preferred_element_type=jnp.float32).reshape(
        row_count, heads_kv, HD
    )
    value_low = (
        jnp.dot(normed, w_value, preferred_element_type=jnp.float32)
        .astype(jnp.bfloat16)
        .reshape(row_count, heads_kv, HD)
    )
    query_low = rotate(query_raw, cos_four, sin_four).astype(jnp.bfloat16)
    key_low = rotate(key_raw, cos_three, sin_three).astype(jnp.bfloat16)
    key_all, value_all = (
        lax.all_gather(key_low, "ctx", axis=0, tiled=True),
        lax.all_gather(value_low, "ctx", axis=0, tiled=True),
    )
    row_top, row_total, out_low = attention_forward(
        query_low, key_all, value_all, segment_row, query_seg, positions
    )
    mixed_low = out_low.reshape(row_count, -1).astype(jnp.bfloat16)
    middle = inputs + head_sum(jnp.dot(mixed_low, w_out, preferred_element_type=jnp.float32))
    scale_second = lax.rsqrt(jnp.mean(middle * middle, axis=-1, keepdims=True) + epsilon)
    normal_second = middle * scale_second
    second = (normal_second * gain_second).astype(jnp.bfloat16)
    gate_part = jnp.dot(second, w_gate, preferred_element_type=jnp.float32)
    upward = jnp.dot(second, w_up, preferred_element_type=jnp.float32)
    sigmoid_gate = jax.nn.sigmoid(gate_part)
    silu_gate = gate_part * sigmoid_gate
    hidden = (silu_gate * upward).astype(jnp.bfloat16)
    result_rows = middle + head_sum(jnp.dot(hidden, w_down, preferred_element_type=jnp.float32))
    output_rows = result_rows.astype(jnp.bfloat16)
    grad_final = grad_in.astype(jnp.float32)
    grad_down = jnp.einsum("tf,td->fd", hidden, grad_in, preferred_element_type=jnp.float32)
    grad_hidden = jnp.einsum("td,fd->tf", grad_in, w_down, preferred_element_type=jnp.float32)
    grad_gate_low = (
        grad_hidden * upward * sigmoid_gate * (1.0 + gate_part * (1.0 - sigmoid_gate))
    ).astype(jnp.bfloat16)
    grad_up_low = (grad_hidden * silu_gate).astype(jnp.bfloat16)
    grad_gate = jnp.einsum("td,tf->df", second, grad_gate_low, preferred_element_type=jnp.float32)
    grad_up = jnp.einsum("td,tf->df", second, grad_up_low, preferred_element_type=jnp.float32)
    grad_second = head_sum(
        jnp.einsum("tf,df->td", grad_gate_low, w_gate, preferred_element_type=jnp.float32)
        + jnp.einsum("tf,df->td", grad_up_low, w_up, preferred_element_type=jnp.float32)
    )
    scaled_second = grad_second * gain_second
    grad_gain_mlp = jnp.sum(grad_second * normal_second, axis=0)
    grad_middle = grad_final + scale_second * (
        scaled_second
        - normal_second * jnp.mean(scaled_second * normal_second, axis=-1, keepdims=True)
    )
    grad_middle_low = grad_middle.astype(jnp.bfloat16)
    grad_out = jnp.einsum(
        "tk,td->kd", mixed_low, grad_middle_low, preferred_element_type=jnp.float32
    )
    grad_mixed = (
        jnp.einsum("td,kd->tk", grad_middle_low, w_out, preferred_element_type=jnp.float32)
        .astype(jnp.bfloat16)
        .reshape(row_count, heads_kv, GROUP, HD)
    )
    row_delta = jnp.transpose(jnp.sum(grad_mixed.astype(jnp.float32) * out_low, axis=-1), (1, 2, 0))
    grad_query_rot, grad_keys, grad_values = attention_backward(
        query_low,
        key_all,
        value_all,
        segment_row,
        query_seg,
        positions,
        row_top,
        row_total,
        grad_mixed,
        row_delta,
    )
    grad_key_mine, grad_value_mine = (
        lax.psum_scatter(
            grad_keys.astype(jnp.bfloat16), "ctx", scatter_dimension=0, tiled=True
        ).astype(jnp.float32),
        lax.psum_scatter(
            grad_values.astype(jnp.bfloat16), "ctx", scatter_dimension=0, tiled=True
        ).astype(jnp.float32),
    )
    grad_query_low = (
        rotate(grad_query_rot, cos_four, -sin_four).astype(jnp.bfloat16).reshape(row_count, -1)
    )
    grad_key_low = (
        rotate(grad_key_mine, cos_three, -sin_three).astype(jnp.bfloat16).reshape(row_count, -1)
    )
    grad_value_low = grad_value_mine.astype(jnp.bfloat16).reshape(row_count, -1)
    grad_query = jnp.einsum("td,tk->dk", normed, grad_query_low, preferred_element_type=jnp.float32)
    grad_key = jnp.einsum("td,tk->dk", normed, grad_key_low, preferred_element_type=jnp.float32)
    grad_value = jnp.einsum("td,tk->dk", normed, grad_value_low, preferred_element_type=jnp.float32)
    grad_normed = head_sum(
        jnp.einsum("tk,dk->td", grad_query_low, w_query, preferred_element_type=jnp.float32)
        + jnp.einsum("tk,dk->td", grad_key_low, w_key, preferred_element_type=jnp.float32)
        + jnp.einsum("tk,dk->td", grad_value_low, w_value, preferred_element_type=jnp.float32)
    )
    scaled_first = grad_normed * gain_first
    grad_gain_attn = jnp.sum(grad_normed * normal_first, axis=0)
    grad_tokens = grad_middle + scale_first * (
        scaled_first - normal_first * jnp.mean(scaled_first * normal_first, axis=-1, keepdims=True)
    )
    gradients = (
        grad_gain_attn,
        grad_query,
        grad_key,
        grad_value,
        grad_gain_mlp,
        grad_gate,
        grad_up,
        grad_out,
        grad_down,
    )
    return (output_rows, grad_tokens, gradients)


def body(
    tokens,
    segments,
    cotangent,
    gain_attn,
    w_query,
    w_key,
    w_value,
    w_out,
    gain_mlp,
    w_gate,
    w_up,
    w_down,
):
    micro_count = tokens.shape[0]
    row_count = tokens.shape[1]
    positions = lax.axis_index("ctx") * row_count + jnp.arange(row_count, dtype=jnp.int32)
    cosine_table, sine_table = rope_tables(positions)
    shards = (gain_attn, w_query, w_key, w_value, gain_mlp, w_gate, w_up, w_out, w_down)
    outputs = []
    token_grads = []
    reduced = tuple((jnp.zeros(tensor_piece.shape, jnp.float32) for tensor_piece in shards))
    for micro_index in range(micro_count):
        gathered = weight_gather(shards)
        output_rows, grad_rows, grads_now = micro_step(
            gathered,
            tokens[micro_index],
            segments[micro_index],
            cotangent[micro_index],
            positions,
            cosine_table,
            sine_table,
        )
        outputs.append(output_rows)
        token_grads.append(grad_rows)
        reduced = tuple(
            (earlier + addend for earlier, addend in zip(reduced, grad_reduce(grads_now)))
        )
    return (
        jnp.stack(outputs),
        jnp.stack(token_grads),
        reduced[0],
        reduced[1],
        reduced[2],
        reduced[3],
        reduced[7],
        reduced[4],
        reduced[5],
        reduced[6],
        reduced[8],
    )


def solution(mesh):
    placed = (
        P("fsdp", "ctx", None),
        P("fsdp", None),
        P("fsdp", "ctx", None),
        P(("fsdp", "ctx")),
        P(("fsdp", "ctx"), "tp"),
        P(("fsdp", "ctx"), "tp"),
        P(("fsdp", "ctx"), "tp"),
        P("tp", ("fsdp", "ctx")),
        P(("fsdp", "ctx")),
        P(("fsdp", "ctx"), "tp"),
        P(("fsdp", "ctx"), "tp"),
        P("tp", ("fsdp", "ctx")),
    )
    return jax.shard_map(
        body,
        mesh=mesh,
        in_specs=placed,
        out_specs=(
            P("fsdp", "ctx", None),
            P("fsdp", "ctx", None),
            P(("fsdp", "ctx")),
            P(("fsdp", "ctx"), "tp"),
            P(("fsdp", "ctx"), "tp"),
            P(("fsdp", "ctx"), "tp"),
            P("tp", ("fsdp", "ctx")),
            P(("fsdp", "ctx")),
            P(("fsdp", "ctx"), "tp"),
            P(("fsdp", "ctx"), "tp"),
            P("tp", ("fsdp", "ctx")),
        ),
        check_vma=False,
    )
```

profile of v0, /device:TPU:0, one launch (start us, length us, event | category | flops | bytes accessed | tf_op | source)
XLA Modules:
  0.0 1458.8 jit_solution(3452239640662511657)
XLA Ops:
  13.7 35.7 %all-reduce.5 = (bf16[1536]{0:T(1024)(128)(2,1)S(1)}, bf16[1536]{0:T(1024)(128)(2,1)S(1)}) all-reduce(bf16[1536]{0:T(1024)(128)(2,1)S(1)} %dynamic-update-slice, bf16[1536]{0:T(1024)(128)(2,1)S(1)} %dynamic-update-slice.1), channel_id=1, replica_groups=mesh['fsdp'=4,'ctx'=4,'tp'=2] {'fsdp','ctx'}, use_global_device_ids=true, to_apply=%add | all-reduce | flops 3072 | bytes 12288
  62.7 28.5 %all-gather.10.cloned.1.call-done = bf16[1536,384]{1,0:T(8,128)(2,1)} async-done(((bf16[96,384]{1,0:T(8,128)(2,1)}), bf16[1536,384]{1,0:T(8,128)(2,1)}) %all-gather.10.cloned.1.call-update) | async-done | bytes 1179664 | tf_op jit(solution)/shard_map/all_gather | solution.py:42
  103.6 9.2 all_gather.50
  112.8 11.0 all_gather.52
  123.8 11.1 all-gather.12.cloned.1.call-done
  143.7 13.0 while.98
  170.1 15.0 %while.96 = (s32[]{:T(128)}, f32[4,2,256]{2,1,0:T(2,128)S(1)}, f32[4,2,256]{2,1,0:T(2,128)S(1)}, s32[256]{0:T(256)S(1)}, s32[1024]{0:T(1024)S(1)}, /*index=5*/bf...) while((s32[]{:T(128)}, f32[4,2,256]{2,1,0:T(2,128)S(1)}, ...), condition=%wide.region_4.5_spmd.clone, body=%wide.region_1.4_spmd.clone.sunk | while | flops 210119424 | bytes 9688262 | solution.py:114
  202.8 48.0 %all-reduce.17.cloned.1.call-done = (bf16[256,1536]{1,0:T(8,128)(2,1)}, bf16[256,1536]{1,0:T(8,128)(2,1)}) async-done(((bf16[256,1536]{1,0:T(8,128)(2,1)}, bf16[256,1536]{1,0:T(8,128)(2,1)}), (bf16[256,1536]{1,0:T(8,128)(2,1)}, bf16[256,1536]{1,0:T(8,128)(2,1)})) %all-reduce.17.cloned.1.call-update) | async-done | bytes 1572880 | tf_op jit(solution)/shard_map/psum | solution.py:35
  254.7 60.5 %all-gather.16.cloned.1.call-done = bf16[1536,2048]{1,0:T(8,128)(2,1)} async-done(((bf16[96,2048]{1,0:T(8,128)(2,1)}), bf16[1536,2048]{1,0:T(8,128)(2,1)}) %all-gather.16.cloned.1.call-update) | async-done | bytes 6291472 | tf_op jit(solution)/shard_map/all_gather | solution.py:45
  321.3 56.9 %all-gather.18.cloned.1.call-done = bf16[1536,2048]{1,0:T(8,128)(2,1)} async-done(((bf16[96,2048]{1,0:T(8,128)(2,1)}), bf16[1536,2048]{1,0:T(8,128)(2,1)}) %all-gather.18.cloned.1.call-update) | async-done | bytes 6291472 | tf_op jit(solution)/shard_map/all_gather | solution.py:46
  390.8 50.4 %all-gather.20.cloned.1.call-done = bf16[2048,1536]{0,1:T(8,128)(2,1)} async-done(((bf16[2048,96]{0,1:T(8,128)(2,1)}), bf16[2048,1536]{0,1:T(8,128)(2,1)}) %all-gather.20.cloned.1.call-update) | async-done | bytes 6291472 | tf_op jit(solution)/shard_map/all_gather | solution.py:50
  466.1 50.3 %all-reduce.15.cloned.1.call-done = (bf16[256,1536]{1,0:T(8,128)(2,1)}, bf16[256,1536]{1,0:T(8,128)(2,1)}) async-done(((bf16[256,1536]{1,0:T(8,128)(2,1)}, bf16[256,1536]{1,0:T(8,128)(2,1)}), (bf16[256,1536]{1,0:T(8,128)(2,1)}, bf16[256,1536]{1,0:T(8,128)(2,1)})) %all-reduce.15.cloned.1.call-update) | async-done | bytes 1572880 | tf_op jit(solution)/shard_map/psum | solution.py:35
  526.6 21.3 %while.100 = (s32[]{:T(128)}, f32[256,4,2,96]{0,3,2,1:T(8,128)}, bf16[1024,4,96]{0,2,1:T(8,128)(2,1)}, bf16[1024,4,96]{0,2,1:T(8,128)(2,1)}, bf16[1024,4,96]{0,2...) while((s32[]{:T(128)}, f32[256,4,2,96]{0,3,2,1:T(8,128)}, ...), condition=%wide.region_24.25_spmd.clone, body=%wide.region_23.24_spmd.clone.sunk | while | flops 1017905920 | bytes 68064656 | solution.py:191
  553.3 21.5 %while.101 = (s32[]{:T(128)}, f32[256,4,2,96]{0,3,2,1:T(8,128)}, bf16[1024,4,96]{0,2,1:T(8,128)(2,1)}, bf16[1024,4,96]{0,2,1:T(8,128)(2,1)}, bf16[1024,4,96]{0,2...) while((s32[]{:T(128)}, f32[256,4,2,96]{0,3,2,1:T(8,128)}, ...), condition=%wide.region_33.0_spmd.clone, body=%wide.region_32.0_spmd.clone.sunk | while | flops 1017905920 | bytes 68064656 | solution.py:191
  605.9 21.1 %reduce-scatter.18.cloned.1.call-done = bf16[256,4,96]{0,2,1:T(8,128)(2,1)} async-done(((bf16[1024,4,96]{0,2,1:T(8,128)(2,1)}), bf16[256,4,96]{0,2,1:T(8,128)(2,1)}) %reduce-scatter.18.cloned.1.call-update) | async-done | bytes 196624 | tf_op jit(solution)/shard_map/reduce_scatter | solution.py:286
  631.1 21.8 %reduce-scatter.14.cloned.1.call-done = bf16[256,4,96]{0,2,1:T(8,128)(2,1)} async-done(((bf16[1024,4,96]{0,2,1:T(8,128)(2,1)}), bf16[256,4,96]{0,2,1:T(8,128)(2,1)}) %reduce-scatter.14.cloned.1.call-update) | async-done | bytes 196624 | tf_op jit(solution)/shard_map/reduce_scatter | solution.py:286
  704.8 37.6 %all-reduce.13.cloned.1.call-done = (bf16[256,1536]{1,0:T(8,128)(2,1)}, bf16[256,1536]{1,0:T(8,128)(2,1)}, bf16[256,1536]{1,0:T(8,128)(2,1)}, bf16[256,1536]{1,0:T(8,128)(2,1)}) async-done(((bf16[256,1536]{1,0:T(8,128)(2,1)}, bf16[256,1536]{1,0:T(8,128)(2,1)}, bf16[256,1536]{1,0:T(8,128)(2,1)}, bf16[256,1536]{1,0:T(8,128)(2,1)}), (bf16[256,1536]{1,0:T(8,128)(2,1)}, bf16[256,1536]{1,0:T(8,128)(2,1)}, ...) | async-done | bytes 3145744 | tf_op jit(solution)/shard_map/psum | solution.py:35
  744.7 61.4 %all-reduce.4 = (f32[1536]{0:T(1024)S(1)}, f32[1536]{0:T(1024)S(1)}) all-reduce(f32[1536]{0:T(1024)S(1)} %add.543, f32[1536]{0:T(1024)S(1)} %add.548), channel_id=15, replica_groups=mesh['fsdp'=4,'ctx'=4,'tp'=2] {'fsdp','ctx'}, use_global_device_ids=true, to_apply=%region_39.40.clone | all-reduce | flops 3072 | bytes 24576
  814.7 61.7 %reduce-scatter.24.cloned.1.call-done = f32[96,384]{1,0:T(8,128)} async-done(((f32[1536,384]{1,0:T(8,128)}), f32[96,384]{1,0:T(8,128)}) %reduce-scatter.24.cloned.1.call-update) | async-done | bytes 147472 | tf_op jit(solution)/shard_map/reduce_scatter | solution.py:60
  876.3 79.4 %reduce-scatter.20.cloned.1.call-done = f32[96,768]{1,0:T(8,128)} async-done(((f32[1536,768]{1,0:T(8,128)}), f32[96,768]{1,0:T(8,128)}) %reduce-scatter.20.cloned.1.call-update) | async-done | bytes 294928 | tf_op jit(solution)/shard_map/reduce_scatter | solution.py:58
  955.8 78.9 %reduce-scatter.26.cloned.1.call-done = f32[768,96]{0,1:T(8,128)} async-done(((f32[768,1536]{0,1:T(8,128)}), f32[768,96]{0,1:T(8,128)}) %reduce-scatter.26.cloned.1.call-update) | async-done | bytes 294928 | tf_op jit(solution)/shard_map/reduce_scatter | solution.py:66
  1034.7 139.0 %reduce-scatter.28.cloned.1.call-done = f32[96,2048]{1,0:T(8,128)} async-done(((f32[1536,2048]{1,0:T(8,128)}), f32[96,2048]{1,0:T(8,128)}) %reduce-scatter.28.cloned.1.call-update) | async-done | bytes 786448 | tf_op jit(solution)/shard_map/reduce_scatter | solution.py:62
  1173.7 138.9 %reduce-scatter.30.cloned.1.call-done = f32[96,2048]{1,0:T(8,128)} async-done(((f32[1536,2048]{1,0:T(8,128)}), f32[96,2048]{1,0:T(8,128)}) %reduce-scatter.30.cloned.1.call-update) | async-done | bytes 786448 | tf_op jit(solution)/shard_map/reduce_scatter | solution.py:63
  1312.6 139.1 %reduce-scatter.32.cloned.1.call-done = f32[2048,96]{0,1:T(8,128)} async-done(((f32[2048,1536]{0,1:T(8,128)}), f32[2048,96]{0,1:T(8,128)}) %reduce-scatter.32.cloned.1.call-update) | async-done | bytes 786448 | tf_op jit(solution)/shard_map/reduce_scatter | solution.py:67
  (464 shorter events, 315.8 us)
Async XLA Ops:
  7.2 45.7 %all-gather.8.cloned.1.call-start = ((), (), s32[]{:S(2)}) async-start(), calls=%async_computation.11 | async-start | bytes 1253376 | tf_op jit(solution)/shard_map/all_gather | solution.py:43
  8.0 83.2 %all-gather.10.cloned.1.call-start = ((), (), s32[]{:S(2)}) async-start(), calls=%async_computation.12 | async-start | bytes 1253376 | tf_op jit(solution)/shard_map/all_gather | solution.py:42
  8.7 126.2 %all-gather.12.cloned.1.call-start = ((), (), s32[]{:S(2)}) async-start(), calls=%async_computation.13 | async-start | bytes 2506752 | tf_op jit(solution)/shard_map/all_gather | solution.py:41
  9.5 185.5 %all-gather.14.cloned.1.call-start = ((), (), s32[]{:S(2)}) async-start(), calls=%async_computation.14 | async-start | bytes 2506752 | tf_op jit(solution)/shard_map/all_gather | solution.py:49
  10.0 240.8 %all-reduce.17.cloned.1.call-start = ((), (), s32[]{:S(2)}) async-start(), calls=%async_computation.31 | async-start | bytes 3145728 | tf_op jit(solution)/shard_map/psum | solution.py:35
  49.4 92.5 %copy-start.60 = (f32[1536]{0:T(1024)}, f32[1536]{0:T(1024)S(1)}, u32[]{:S(2)}) copy-start(f32[1536]{0:T(1024)S(1)} %convert_element_type.311) | copy-start | bytes 18436
  52.1 89.8 %copy-start.75 = (f32[256]{0:T(256)}, f32[256]{0:T(256)S(1)}, u32[]{:S(2)}) copy-start(f32[256]{0:T(256)S(1)} %get-tuple-element.1604) | copy-start | bytes 3076
  52.9 89.9 %copy-start.51 = (f32[256,48]{0,1:T(8,128)}, f32[256,48]{0,1:T(8,128)S(1)}, u32[]{:S(2)}) copy-start(f32[256,48]{0,1:T(8,128)S(1)} %get-tuple-element.1601) | copy-start | bytes 147460
  200.3 114.9 %all-gather.16.cloned.1.call-start = ((), (), s32[]{:S(2)}) async-start(), calls=%async_computation.15 | async-start | bytes 6684672 | tf_op jit(solution)/shard_map/all_gather | solution.py:45
  200.8 177.3 %all-gather.18.cloned.1.call-start = ((), (), s32[]{:S(2)}) async-start(), calls=%async_computation.16 | async-start | bytes 6684672 | tf_op jit(solution)/shard_map/all_gather | solution.py:46
  201.6 239.6 %all-gather.20.cloned.1.call-start = ((), (), s32[]{:S(2)}) async-start(), calls=%async_computation.17 | async-start | bytes 6684672 | tf_op jit(solution)/shard_map/all_gather | solution.py:50
  202.3 314.1 %all-reduce.15.cloned.1.call-start = ((), (), s32[]{:S(2)}) async-start(), calls=%async_computation.30 | async-start | bytes 3145728 | tf_op jit(solution)/shard_map/psum | solution.py:35
  466.0 127.2 %reduce-scatter.12.cloned.1.call-start = ((), (), s32[]{:S(2)}) async-start(), calls=%async_computation.18 | async-start | bytes 983040 | tf_op jit(solution)/shard_map/reduce_scatter | solution.py:283
  551.3 50.0 %reduce-scatter.16.cloned.1.call-start = ((), (), s32[]{:S(2)}) async-start(), calls=%async_computation.20 | async-start | bytes 983040 | tf_op jit(solution)/shard_map/reduce_scatter | solution.py:283
  574.8 52.1 %reduce-scatter.18.cloned.1.call-start = ((), (), s32[]{:S(2)}) async-start(), calls=%async_computation.21 | async-start | bytes 983040 | tf_op jit(solution)/shard_map/reduce_scatter | solution.py:286
  575.4 77.5 %reduce-scatter.14.cloned.1.call-start = ((), (), s32[]{:S(2)}) async-start(), calls=%async_computation.19 | async-start | bytes 983040 | tf_op jit(solution)/shard_map/reduce_scatter | solution.py:286
  587.8 154.6 %all-reduce.13.cloned.1.call-start = ((), (), s32[]{:S(2)}) async-start(), calls=%async_computation.29 | async-start | bytes 6291456 | tf_op jit(solution)/shard_map/psum | solution.py:35
  655.9 158.8 %reduce-scatter.22.cloned.1.call-start = ((), (), s32[]{:S(2)}) async-start(), calls=%async_computation.23 | async-start | bytes 2506752 | tf_op jit(solution)/shard_map/reduce_scatter | solution.py:59
  660.1 216.2 %reduce-scatter.24.cloned.1.call-start = ((), (), s32[]{:S(2)}) async-start(), calls=%async_computation.24 | async-start | bytes 2506752 | tf_op jit(solution)/shard_map/reduce_scatter | solution.py:60
  663.8 291.9 %reduce-scatter.20.cloned.1.call-start = ((), (), s32[]{:S(2)}) async-start(), calls=%async_computation.22 | async-start | bytes 5013504 | tf_op jit(solution)/shard_map/reduce_scatter | solution.py:58
  667.9 366.7 %reduce-scatter.26.cloned.1.call-start = ((), (), s32[]{:S(2)}) async-start(), calls=%async_computation.25 | async-start | bytes 5013504 | tf_op jit(solution)/shard_map/reduce_scatter | solution.py:66
  674.0 499.7 %reduce-scatter.28.cloned.1.call-start = ((), (), s32[]{:S(2)}) async-start(), calls=%async_computation.26 | async-start | bytes 13369344 | tf_op jit(solution)/shard_map/reduce_scatter | solution.py:62
  683.9 628.7 %reduce-scatter.30.cloned.1.call-start = ((), (), s32[]{:S(2)}) async-start(), calls=%async_computation.27 | async-start | bytes 13369344 | tf_op jit(solution)/shard_map/reduce_scatter | solution.py:63
  693.9 757.8 %reduce-scatter.32.cloned.1.call-start = ((), (), s32[]{:S(2)}) async-start(), calls=%async_computation.28 | async-start | bytes 13369344 | tf_op jit(solution)/shard_map/reduce_scatter | solution.py:67
  (100 other events, 545.0 us)
Sparse Core Ops, SparseCore 0:
  10.3 41.1 all-gather.7
  53.9 37.2 all-gather.9
  93.5 41.3 all-gather.11
  137.0 40.9 all-gather.13
  200.4 50.4 all-reduce.16
  253.2 61.8 all-gather.15
  317.7 60.4 all-gather.17
  380.7 60.4 all-gather.19
  466.2 50.2 all-reduce.14
  551.4 23.2 reduce-scatter.11
  578.0 23.2 reduce-scatter.15
  603.6 23.2 reduce-scatter.17
  629.6 23.2 reduce-scatter.13
  656.0 86.3 all-reduce.12
  747.0 63.0 reduce-scatter.21
  814.3 61.9 reduce-scatter.23
  881.1 74.6 reduce-scatter.19
  960.1 74.5 reduce-scatter.25
  1039.8 133.7 reduce-scatter.27
  1178.7 133.8 reduce-scatter.29
  1317.8 133.8 reduce-scatter.31
where the time goes:
time: 1460 us
  waiting for transfers between devices  1030 us (71%)
  matrix products  189 us (13%)
  blocking collectives  134 us (9%)
  other arithmetic  47.7 us (3%)
  local copies, waits for them, and re-layouts  32.6 us (2%)
  between operations  18.9 us (1%)
    reduce_scatter x1, waiting for transfers between devices, grad_reduce(): lax.psum_scatter(gradients[8], ('fsdp', 'ctx'), scatter_dimension=1, tile...  139 us
    reduce_scatter x1, waiting for transfers between devices, grad_reduce(): lax.psum_scatter(gradients[5], ('fsdp', 'ctx'), scatter_dimension=0, tile...  139 us
    reduce_scatter x1, waiting for transfers between devices, grad_reduce(): lax.psum_scatter(gradients[6], ('fsdp', 'ctx'), scatter_dimension=0, tile...  139 us
    psum x3, waiting for transfers between devices, head_sum(): return lax.psum(partial_rows.astype(jnp.bfloat16), 'tp').astype(jnp.float32)  136 us
    unnamed x2, blocking collectives  97.1 us
    reduce_scatter x1, waiting for transfers between devices, grad_reduce(): lax.psum_scatter(gradients[1], ('fsdp', 'ctx'), scatter_dimension=0, tile...  79.4 us
    reduce_scatter x1, waiting for transfers between devices, grad_reduce(): lax.psum_scatter(gradients[7], ('fsdp', 'ctx'), scatter_dimension=1, tile...  78.9 us
    reduce_scatter x1, waiting for transfers between devices, grad_reduce(): lax.psum_scatter(gradients[3], ('fsdp', 'ctx'), scatter_dimension=0, tile...  61.7 us
  transfers between devices with their start and end apart: 21, of which 17 were waited for; matrix products, arithmetic and copies ran while one was open for 13% of the time, Pallas kernels for 0%

commit v1 on v0

--- a/solution.py
+++ b/solution.py
@@ -342,9 +342,9 @@
     shards = (gain_attn, w_query, w_key, w_value, gain_mlp, w_gate, w_up, w_out, w_down)
     outputs = []
     token_grads = []
-    reduced = tuple((jnp.zeros(tensor_piece.shape, jnp.float32) for tensor_piece in shards))
+    gathered = weight_gather(shards)
+    totals = None
     for micro_index in range(micro_count):
-        gathered = weight_gather(shards)
         output_rows, grad_rows, grads_now = micro_step(
             gathered,
             tokens[micro_index],
@@ -356,9 +356,15 @@
         )
         outputs.append(output_rows)
         token_grads.append(grad_rows)
-        reduced = tuple(
-            (earlier + addend for earlier, addend in zip(reduced, grad_reduce(grads_now)))
-        )
+        totals = (
+            grads_now
+            if totals is None
+            else tuple(earlier + addend for earlier, addend in zip(totals, grads_now))
+        )
+    reduced = tuple(
+        tensor_piece.astype(jnp.float32)
+        for tensor_piece in grad_reduce(tuple(total.astype(jnp.bfloat16) for total in totals))
+    )
     return (
         jnp.stack(outputs),
         jnp.stack(token_grads),

time: 1460 us -> 1280 us (0.88)
  waiting for transfers between devices: 1030 us -> 877 us
  blocking collectives: 134 us -> 106 us
    reduce_scatter x1, waiting for transfers between devices: 139 us -> 45.1 us  [grad_reduce(): lax.psum_scatter(gradients[5], ('fsdp', 'ctx'), scatter_dimension=0, tile...]
    reduce_scatter x1, waiting for transfers between devices: 139 us -> 86.2 us  [grad_reduce(): lax.psum_scatter(gradients[6], ('fsdp', 'ctx'), scatter_dimension=0, tile...]
    reduce_scatter x1, waiting for transfers between devices: 139 us -> 87 us  [grad_reduce(): lax.psum_scatter(gradients[8], ('fsdp', 'ctx'), scatter_dimension=1, tile...]
    psum x3, waiting for transfers between devices: 136 us -> 185 us  [head_sum(): return lax.psum(partial_rows.astype(jnp.bfloat16), 'tp').astype(jnp.float32)]
    unnamed x2, blocking collectives: 97.1 us -> 69.4 us
    reduce_scatter x2, waiting for transfers between devices: 6.08 us -> 23.8 us  [micro_step(): lax.psum_scatter(grad_keys.astype(jnp.bfloat16), 'ctx', scatter_dimension...]
    reduce_scatter x1, waiting for transfers between devices: 79.4 us -> 64.7 us  [grad_reduce(): lax.psum_scatter(gradients[1], ('fsdp', 'ctx'), scatter_dimension=0, tile...]
  transfers between devices with their start and end apart: 21 -> 21, of which waited for: 17 -> 18; matrix products, arithmetic and copies ran while one was open for 13% -> 15% of each run, Pallas kernels for 0% -> 0%
where the time goes in v1:
time: 1280 us; the launch traced here: 1270 us
  waiting for transfers between devices  877 us (69%)
  matrix products  179 us (14%)
  blocking collectives  106 us (8%)
  other arithmetic  58.5 us (5%)
  local copies, waits for them, and re-layouts  29.8 us (2%)
  between operations  19 us (1%)
    psum x3, waiting for transfers between devices, head_sum(): return lax.psum(partial_rows.astype(jnp.bfloat16), 'tp').astype(jnp.float32)  185 us
    reduce_scatter x1, waiting for transfers between devices, grad_reduce(): lax.psum_scatter(gradients[8], ('fsdp', 'ctx'), scatter_dimension=1, tile...  87 us
    reduce_scatter x1, waiting for transfers between devices, grad_reduce(): lax.psum_scatter(gradients[6], ('fsdp', 'ctx'), scatter_dimension=0, tile...  86.2 us
    unnamed x2, blocking collectives  69.4 us
    reduce_scatter x1, waiting for transfers between devices, grad_reduce(): lax.psum_scatter(gradients[1], ('fsdp', 'ctx'), scatter_dimension=0, tile...  64.7 us
    reduce_scatter x1, waiting for transfers between devices, grad_reduce(): lax.psum_scatter(gradients[7], ('fsdp', 'ctx'), scatter_dimension=1, tile...  64.4 us
    all_gather x1, waiting for transfers between devices, weight_gather(): lax.all_gather(shards[5], ('fsdp', 'ctx'), axis=0, tiled=True)  60.5 us
    reduce_scatter x1, waiting for transfers between devices, grad_reduce(): lax.psum_scatter(gradients[3], ('fsdp', 'ctx'), scatter_dimension=0, tile...  59 us
  transfers between devices with their start and end apart: 21, of which 18 were waited for; matrix products, arithmetic and copies ran while one was open for 15% of the time, Pallas kernels for 0%

profile of v1, /device:TPU:0, one launch (start us, length us, event | category | flops | bytes accessed | tf_op | source)
XLA Modules:
  0.0 1272.1 jit_solution(5355008559296787262)
XLA Ops:
  13.7 35.7 %all-reduce.5 = (bf16[1536]{0:T(1024)(128)(2,1)S(1)}, bf16[1536]{0:T(1024)(128)(2,1)S(1)}) all-reduce(bf16[1536]{0:T(1024)(128)(2,1)S(1)} %dynamic-update-slice, bf16[1536]{0:T(1024)(128)(2,1)S(1)} %dynamic-update-slice.1), channel_id=1, replica_groups=mesh['fsdp'=4,'ctx'=4,'tp'=2] {'fsdp','ctx'}, use_global_device_ids=true, to_apply=%add | all-reduce | flops 3072 | bytes 12288
  62.7 28.5 %all-gather.10.cloned.1.call-done = bf16[1536,384]{1,0:T(8,128)(2,1)} async-done(((bf16[96,384]{1,0:T(8,128)(2,1)}), bf16[1536,384]{1,0:T(8,128)(2,1)}) %all-gather.10.cloned.1.call-update) | async-done | bytes 1179664 | tf_op jit(solution)/shard_map/all_gather | solution.py:42
  112.8 11.0 all_gather.43
  123.8 11.1 all-gather.12.cloned.1.call-done
  143.7 13.0 %while.98 = (s32[]{:T(128)}, f32[4,2,256]{2,1,0:T(2,128)S(1)}, f32[4,2,256]{2,1,0:T(2,128)S(1)}, s32[256]{0:T(256)S(1)}, s32[1024]{0:T(1024)S(1)}, /*index=5*/bf...) while((s32[]{:T(128)}, f32[4,2,256]{2,1,0:T(2,128)S(1)}, ...), condition=%wide.region_14.15_spmd.clone, body=%wide.region_11.14_spmd.clone.sunk | while | flops 210119424 | bytes 9688262 | solution.py:114
  170.2 15.0 %while.96 = (s32[]{:T(128)}, f32[4,2,256]{2,1,0:T(2,128)S(1)}, f32[4,2,256]{2,1,0:T(2,128)S(1)}, s32[256]{0:T(256)S(1)}, s32[1024]{0:T(1024)S(1)}, /*index=5*/bf...) while((s32[]{:T(128)}, f32[4,2,256]{2,1,0:T(2,128)S(1)}, ...), condition=%wide.region_4.5_spmd.clone, body=%wide.region_1.4_spmd.clone.sunk | while | flops 210119424 | bytes 9688262 | solution.py:114
  202.9 48.0 %all-reduce.17.cloned.1.call-done = (bf16[256,1536]{1,0:T(8,128)(2,1)}, bf16[256,1536]{1,0:T(8,128)(2,1)}) async-done(((bf16[256,1536]{1,0:T(8,128)(2,1)}, bf16[256,1536]{1,0:T(8,128)(2,1)}), (bf16[256,1536]{1,0:T(8,128)(2,1)}, bf16[256,1536]{1,0:T(8,128)(2,1)})) %all-reduce.17.cloned.1.call-update) | async-done | bytes 1572880 | tf_op jit(solution)/shard_map/psum | solution.py:35
  254.7 60.5 %all-gather.16.cloned.1.call-done = bf16[1536,2048]{1,0:T(8,128)(2,1)} async-done(((bf16[96,2048]{1,0:T(8,128)(2,1)}), bf16[1536,2048]{1,0:T(8,128)(2,1)}) %all-gather.16.cloned.1.call-update) | async-done | bytes 6291472 | tf_op jit(solution)/shard_map/all_gather | solution.py:45
  321.3 56.9 %all-gather.18.cloned.1.call-done = bf16[1536,2048]{1,0:T(8,128)(2,1)} async-done(((bf16[96,2048]{1,0:T(8,128)(2,1)}), bf16[1536,2048]{1,0:T(8,128)(2,1)}) %all-gather.18.cloned.1.call-update) | async-done | bytes 6291472 | tf_op jit(solution)/shard_map/all_gather | solution.py:46
  390.8 50.4 %all-gather.20.cloned.1.call-done = bf16[2048,1536]{0,1:T(8,128)(2,1)} async-done(((bf16[2048,96]{0,1:T(8,128)(2,1)}), bf16[2048,1536]{0,1:T(8,128)(2,1)}) %all-gather.20.cloned.1.call-update) | async-done | bytes 6291472 | tf_op jit(solution)/shard_map/all_gather | solution.py:50
  466.2 50.3 %all-reduce.15.cloned.1.call-done = (bf16[256,1536]{1,0:T(8,128)(2,1)}, bf16[256,1536]{1,0:T(8,128)(2,1)}) async-done(((bf16[256,1536]{1,0:T(8,128)(2,1)}, bf16[256,1536]{1,0:T(8,128)(2,1)}), (bf16[256,1536]{1,0:T(8,128)(2,1)}, bf16[256,1536]{1,0:T(8,128)(2,1)})) %all-reduce.15.cloned.1.call-update) | async-done | bytes 1572880 | tf_op jit(solution)/shard_map/psum | solution.py:35
  526.8 21.3 %while.100 = (s32[]{:T(128)}, f32[256,4,2,96]{0,3,2,1:T(8,128)}, bf16[1024,4,96]{0,2,1:T(8,128)(2,1)}, bf16[1024,4,96]{0,2,1:T(8,128)(2,1)}, bf16[1024,4,96]{0,2...) while((s32[]{:T(128)}, f32[256,4,2,96]{0,3,2,1:T(8,128)}, ...), condition=%wide.region_24.0_spmd.clone, body=%wide.region_23.0_spmd.clone.sunk | while | flops 1017905920 | bytes 68064656 | solution.py:191
  553.5 21.3 %while.101 = (s32[]{:T(128)}, f32[256,4,2,96]{0,3,2,1:T(8,128)}, bf16[1024,4,96]{0,2,1:T(8,128)(2,1)}, bf16[1024,4,96]{0,2,1:T(8,128)(2,1)}, bf16[1024,4,96]{0,2...) while((s32[]{:T(128)}, f32[256,4,2,96]{0,3,2,1:T(8,128)}, ...), condition=%wide.region_33.34_spmd.clone, body=%wide.region_32.33_spmd.clone.sunk | while | flops 1017905920 | bytes 68064656 | solution.py:191
  577.6 23.8 %reduce-scatter.16.cloned.1.call-done = bf16[256,4,96]{0,2,1:T(8,128)(2,1)} async-done(((bf16[1024,4,96]{0,2,1:T(8,128)(2,1)}), bf16[256,4,96]{0,2,1:T(8,128)(2,1)}) %reduce-scatter.16.cloned.1.call-update) | async-done | bytes 196624 | tf_op jit(solution)/shard_map/reduce_scatter | solution.py:283
  605.3 22.5 %reduce-scatter.14.cloned.1.call-done = bf16[256,4,96]{0,2,1:T(8,128)(2,1)} async-done(((bf16[1024,4,96]{0,2,1:T(8,128)(2,1)}), bf16[256,4,96]{0,2,1:T(8,128)(2,1)}) %reduce-scatter.14.cloned.1.call-update) | async-done | bytes 196624 | tf_op jit(solution)/shard_map/reduce_scatter | solution.py:286
  630.7 22.9 %reduce-scatter.18.cloned.1.call-done = bf16[256,4,96]{0,2,1:T(8,128)(2,1)} async-done(((bf16[1024,4,96]{0,2,1:T(8,128)(2,1)}), bf16[256,4,96]{0,2,1:T(8,128)(2,1)}) %reduce-scatter.18.cloned.1.call-update) | async-done | bytes 196624 | tf_op jit(solution)/shard_map/reduce_scatter | solution.py:286
  716.7 59.0 %reduce-scatter.24.cloned.1.call-done = bf16[96,384]{1,0:T(8,128)(2,1)} async-done(((bf16[1536,384]{1,0:T(8,128)(2,1)}), bf16[96,384]{1,0:T(8,128)(2,1)}) %reduce-scatter.24.cloned.1.call-update) | async-done | bytes 73744 | tf_op jit(solution)/shard_map/reduce_scatter | solution.py:60
  777.3 64.7 %reduce-scatter.20.cloned.1.call-done = bf16[96,768]{1,0:T(8,128)(2,1)} async-done(((bf16[1536,768]{1,0:T(8,128)(2,1)}), bf16[96,768]{1,0:T(8,128)(2,1)}) %reduce-scatter.20.cloned.1.call-update) | async-done | bytes 147472 | tf_op jit(solution)/shard_map/reduce_scatter | solution.py:58
  843.7 64.4 %reduce-scatter.26.cloned.1.call-done = bf16[768,96]{0,1:T(8,128)(2,1)} async-done(((bf16[768,1536]{0,1:T(8,128)(2,1)}), bf16[768,96]{0,1:T(8,128)(2,1)}) %reduce-scatter.26.cloned.1.call-update) | async-done | bytes 147472 | tf_op jit(solution)/shard_map/reduce_scatter | solution.py:66
  909.7 86.6 %all-reduce.13.cloned.1.call-done = (bf16[256,1536]{1,0:T(8,128)(2,1)}, bf16[256,1536]{1,0:T(8,128)(2,1)}, bf16[256,1536]{1,0:T(8,128)(2,1)}, bf16[256,1536]{1,0:T(8,128)(2,1)}) async-done(((bf16[256,1536]{1,0:T(8,128)(2,1)}, bf16[256,1536]{1,0:T(8,128)(2,1)}, bf16[256,1536]{1,0:T(8,128)(2,1)}, bf16[256,1536]{1,0:T(8,128)(2,1)}), (bf16[256,1536]{1,0:T(8,128)(2,1)}, bf16[256,1536]{1,0:T(8,128)(2,1)}, ...) | async-done | bytes 3145744 | tf_op jit(solution)/shard_map/psum | solution.py:35
  998.7 33.7 %all-reduce.4 = (bf16[1536]{0:T(1024)(128)(2,1)S(1)}, bf16[1536]{0:T(1024)(128)(2,1)S(1)}) all-reduce(bf16[1536]{0:T(1024)(128)(2,1)S(1)} %add_convert_fusion.12, bf16[1536]{0:T(1024)(128)(2,1)S(1)} %add_convert_fusion.11), channel_id=6, replica_groups=mesh['fsdp'=4,'ctx'=4,'tp'=2] {'fsdp','ctx'}, use_global_device_ids=true, to_apply=%region_40.41.clone | all-reduce | flops 3072 | bytes 12288
  1040.9 45.1 %reduce-scatter.28.cloned.1.call-done = bf16[96,2048]{1,0:T(8,128)(2,1)} async-done(((bf16[1536,2048]{1,0:T(8,128)(2,1)}), bf16[96,2048]{1,0:T(8,128)(2,1)}) %reduce-scatter.28.cloned.1.call-update) | async-done | bytes 393232 | tf_op jit(solution)/shard_map/reduce_scatter | solution.py:62
  1088.0 86.2 %reduce-scatter.30.cloned.1.call-done = bf16[96,2048]{1,0:T(8,128)(2,1)} async-done(((bf16[1536,2048]{1,0:T(8,128)(2,1)}), bf16[96,2048]{1,0:T(8,128)(2,1)}) %reduce-scatter.30.cloned.1.call-update) | async-done | bytes 393232 | tf_op jit(solution)/shard_map/reduce_scatter | solution.py:63
  1176.1 87.0 %reduce-scatter.32.cloned.1.call-done = bf16[2048,96]{0,1:T(8,128)(2,1)} async-done(((bf16[2048,1536]{0,1:T(8,128)(2,1)}), bf16[2048,96]{0,1:T(8,128)(2,1)}) %reduce-scatter.32.cloned.1.call-update) | async-done | bytes 393232 | tf_op jit(solution)/shard_map/reduce_scatter | solution.py:67
  (469 shorter events, 321.1 us)
Async XLA Ops:
  7.2 45.7 %all-gather.8.cloned.1.call-start = ((), (), s32[]{:S(2)}) async-start(), calls=%async_computation.11 | async-start | bytes 1253376 | tf_op jit(solution)/shard_map/all_gather | solution.py:43
  8.0 83.2 %all-gather.10.cloned.1.call-start = ((), (), s32[]{:S(2)}) async-start(), calls=%async_computation.12 | async-start | bytes 1253376 | tf_op jit(solution)/shard_map/all_gather | solution.py:42
  8.7 126.2 %all-gather.12.cloned.1.call-start = ((), (), s32[]{:S(2)}) async-start(), calls=%async_computation.13 | async-start | bytes 2506752 | tf_op jit(solution)/shard_map/all_gather | solution.py:41
  9.5 185.6 %all-gather.14.cloned.1.call-start = ((), (), s32[]{:S(2)}) async-start(), calls=%async_computation.14 | async-start | bytes 2506752 | tf_op jit(solution)/shard_map/all_gather | solution.py:49
  10.0 240.9 %all-reduce.17.cloned.1.call-start = ((), (), s32[]{:S(2)}) async-start(), calls=%async_computation.31 | async-start | bytes 3145728 | tf_op jit(solution)/shard_map/psum | solution.py:35
  49.4 92.5 %copy-start.59 = (f32[1536]{0:T(1024)}, f32[1536]{0:T(1024)S(1)}, u32[]{:S(2)}) copy-start(f32[1536]{0:T(1024)S(1)} %convert_element_type.365) | copy-start | bytes 18436
  52.1 89.8 %copy-start.74 = (f32[256]{0:T(256)}, f32[256]{0:T(256)S(1)}, u32[]{:S(2)}) copy-start(f32[256]{0:T(256)S(1)} %get-tuple-element.1604) | copy-start | bytes 3076
  52.9 89.9 %copy-start.50 = (f32[256,48]{0,1:T(8,128)}, f32[256,48]{0,1:T(8,128)S(1)}, u32[]{:S(2)}) copy-start(f32[256,48]{0,1:T(8,128)S(1)} %get-tuple-element.1601) | copy-start | bytes 147460
  200.3 114.9 %all-gather.16.cloned.1.call-start = ((), (), s32[]{:S(2)}) async-start(), calls=%async_computation.15 | async-start | bytes 6684672 | tf_op jit(solution)/shard_map/all_gather | solution.py:45
  200.9 177.3 %all-gather.18.cloned.1.call-start = ((), (), s32[]{:S(2)}) async-start(), calls=%async_computation.16 | async-start | bytes 6684672 | tf_op jit(solution)/shard_map/all_gather | solution.py:46
  201.6 239.6 %all-gather.20.cloned.1.call-start = ((), (), s32[]{:S(2)}) async-start(), calls=%async_computation.17 | async-start | bytes 6684672 | tf_op jit(solution)/shard_map/all_gather | solution.py:50
  202.4 314.1 %all-reduce.15.cloned.1.call-start = ((), (), s32[]{:S(2)}) async-start(), calls=%async_computation.30 | async-start | bytes 3145728 | tf_op jit(solution)/shard_map/psum | solution.py:35
  466.1 110.4 %reduce-scatter.12.cloned.1.call-start = ((), (), s32[]{:S(2)}) async-start(), calls=%async_computation.18 | async-start | bytes 983040 | tf_op jit(solution)/shard_map/reduce_scatter | solution.py:283
  551.5 50.0 %reduce-scatter.16.cloned.1.call-start = ((), (), s32[]{:S(2)}) async-start(), calls=%async_computation.20 | async-start | bytes 983040 | tf_op jit(solution)/shard_map/reduce_scatter | solution.py:283
  574.9 52.9 %reduce-scatter.14.cloned.1.call-start = ((), (), s32[]{:S(2)}) async-start(), calls=%async_computation.19 | async-start | bytes 983040 | tf_op jit(solution)/shard_map/reduce_scatter | solution.py:286
  575.4 78.2 %reduce-scatter.18.cloned.1.call-start = ((), (), s32[]{:S(2)}) async-start(), calls=%async_computation.21 | async-start | bytes 983040 | tf_op jit(solution)/shard_map/reduce_scatter | solution.py:286
  576.2 139.0 %reduce-scatter.22.cloned.1.call-start = ((), (), s32[]{:S(2)}) async-start(), calls=%async_computation.23 | async-start | bytes 1253376 | tf_op jit(solution)/shard_map/reduce_scatter | solution.py:59
  605.2 170.5 %reduce-scatter.24.cloned.1.call-start = ((), (), s32[]{:S(2)}) async-start(), calls=%async_computation.24 | async-start | bytes 1253376 | tf_op jit(solution)/shard_map/reduce_scatter | solution.py:60
  657.3 184.8 %reduce-scatter.20.cloned.1.call-start = ((), (), s32[]{:S(2)}) async-start(), calls=%async_computation.22 | async-start | bytes 2506752 | tf_op jit(solution)/shard_map/reduce_scatter | solution.py:58
  662.0 246.1 %reduce-scatter.26.cloned.1.call-start = ((), (), s32[]{:S(2)}) async-start(), calls=%async_computation.25 | async-start | bytes 2506752 | tf_op jit(solution)/shard_map/reduce_scatter | solution.py:66
  667.6 328.7 %all-reduce.13.cloned.1.call-start = ((), (), s32[]{:S(2)}) async-start(), calls=%async_computation.29 | async-start | bytes 6291456 | tf_op jit(solution)/shard_map/psum | solution.py:35
  687.4 398.7 %reduce-scatter.28.cloned.1.call-start = ((), (), s32[]{:S(2)}) async-start(), calls=%async_computation.26 | async-start | bytes 6684672 | tf_op jit(solution)/shard_map/reduce_scatter | solution.py:62
  695.4 478.8 %reduce-scatter.30.cloned.1.call-start = ((), (), s32[]{:S(2)}) async-start(), calls=%async_computation.27 | async-start | bytes 6684672 | tf_op jit(solution)/shard_map/reduce_scatter | solution.py:63
  703.7 559.5 %reduce-scatter.32.cloned.1.call-start = ((), (), s32[]{:S(2)}) async-start(), calls=%async_computation.28 | async-start | bytes 6684672 | tf_op jit(solution)/shard_map/reduce_scatter | solution.py:67
  (99 other events, 633.8 us)
Sparse Core Ops, SparseCore 0:
  10.3 41.1 all-gather.7
  53.8 37.3 all-gather.9
  93.5 41.3 all-gather.11
  137.0 40.9 all-gather.13
  200.4 50.4 all-reduce.16
  253.3 61.8 all-gather.15
  317.7 60.4 all-gather.17
  380.7 60.4 all-gather.19
  466.2 50.2 all-reduce.14
  551.6 23.2 reduce-scatter.11
  578.1 23.2 reduce-scatter.15
  604.4 23.2 reduce-scatter.13
  630.4 23.2 reduce-scatter.17
  657.2 57.9 reduce-scatter.21
  718.6 57.0 reduce-scatter.23
  779.9 62.0 reduce-scatter.19
  846.1 61.9 reduce-scatter.25
  911.0 85.3 all-reduce.12
  1000.8 85.2 reduce-scatter.27
  1089.8 84.3 reduce-scatter.29
  1178.7 84.4 reduce-scatter.31

commit v2 on v1

--- a/solution.py
+++ b/solution.py
@@ -3,6 +3,8 @@
 import jax
 import jax.numpy as jnp
 from jax import lax
+from jax.experimental import pallas as pl
+from jax.experimental.pallas import tpu as pltpu
 from jax.sharding import PartitionSpec as P
 
 HD = 96
@@ -380,6 +382,1181 @@
     )
 
 
+MESH = pl.DeviceIdType.MESH
+UNIT = 384
+ROWS = 512
+SPAN = 256
+WIDE = 1536
+F32 = jnp.float32
+BF16 = jnp.bfloat16
+NT = (((1,), (1,)), ((), ()))
+TN = (((0,), (0,)), ((), ()))
+
+
+def dot_nn(a, b):
+    return jnp.dot(a, b, preferred_element_type=F32)
+
+
+def dot_nt(a, b):
+    return lax.dot_general(a, b, NT, preferred_element_type=F32)
+
+
+def dot_tn(a, b):
+    return lax.dot_general(a, b, TN, preferred_element_type=F32)
+
+
+class Place:
+    def __init__(self):
+        f, c, t = (lax.axis_index(axis) for axis in ("fsdp", "ctx", "tp"))
+        self.f, self.c, self.t = f, c, t
+        self.y, self.k = lax.div(c, 2), lax.rem(c, 2)
+        self.oy, self.ok = 1 - self.y, 1 - self.k
+        self.half = lax.div(f, 2)
+        self.inner = (f == 1) | (f == 2)
+        self.edge = (f == 0) | (f == 3)
+        self.near_f = f + 1 - 2 * lax.rem(f, 2)
+        self.mid_f = 2 - self.half
+        self.far_f = 3 - 3 * self.half
+        self.near = (self.near_f, c, t)
+        self.mid = (self.mid_f, c, t)
+        self.far = (self.far_f, c, t)
+        self.ypeer = (f, c + 2 - 4 * self.y, t)
+        self.sib = (f, c + 1 - 2 * self.k, t)
+        self.xpeer = (f, c, 1 - t)
+
+    def barrier(self):
+        sem = pltpu.get_barrier_semaphore()
+        others = [(lax.rem(self.f + step, 4), self.c, self.t) for step in (1, 2, 3)]
+        others += [self.ypeer, self.sib, self.xpeer]
+        for other in others:
+            pl.semaphore_signal(sem, inc=1, device_id=other, device_id_type=MESH)
+        pl.semaphore_wait(sem, len(others))
+
+
+def remote(src, dst, send, recv, device):
+    return pltpu.make_async_remote_copy(
+        src_ref=src,
+        dst_ref=dst,
+        send_sem=send,
+        recv_sem=recv,
+        device_id=device,
+        device_id_type=MESH,
+    )
+
+
+def lanes(rows, columns):
+    return lax.broadcasted_iota(jnp.int32, (rows, columns), 1)
+
+
+def unpack_heads(x):
+    lane = lanes(x.shape[0], 128)
+    one, two, three = x[:, :128], x[:, 128:256], x[:, 256:]
+    heads = (
+        one,
+        pltpu.roll(jnp.where(lane < 64, two, one), 32, 1),
+        pltpu.roll(jnp.where(lane < 32, three, two), 64, 1),
+        pltpu.roll(three, 96, 1),
+    )
+    return [jnp.where(lane < HD, head, 0.0) for head in heads]
+
+
+def pack_heads(heads):
+    lane = lanes(heads[0].shape[0], 128)
+    second = pltpu.roll(heads[1], 96, 1)
+    third = pltpu.roll(heads[2], 64, 1)
+    fourth = pltpu.roll(heads[3], 32, 1)
+    return jnp.concatenate(
+        [
+            jnp.where(lane < 96, heads[0], second),
+            jnp.where(lane < 64, second, third),
+            jnp.where(lane < 32, third, fourth),
+        ],
+        axis=1,
+    )
+
+
+def turn(x, cosine, sine):
+    lane = lax.rem(lanes(x.shape[0], UNIT), HD)
+    swapped = jnp.where(lane < HD // 2, pltpu.roll(x, UNIT - HD // 2, 1), pltpu.roll(x, HD // 2, 1))
+    return x * cosine + swapped * sine
+
+
+def transpose_into(dst, src):
+    @pl.loop(0, WIDE // 128)
+    def _(i):
+        at = pl.multiple_of(i * 128, 128)
+        dst[pl.ds(at, 128), :] = src[:, pl.ds(at, 128)].astype(F32).T.astype(BF16)
+
+
+def weight(buf, slot, lo, hi):
+    return buf[slot, :, :, :, :, lo:hi].reshape(WIDE, hi - lo)
+
+
+def allowed_keys(low_row, high_row):
+    row = lax.broadcasted_iota(jnp.int32, (4 * SPAN, SPAN), 0)
+    return (row >= low_row) & (row <= high_row)
+
+
+def forward_kernel(
+    packed,
+    gains,
+    tokens,
+    cot,
+    cosine,
+    sine,
+    low,
+    high,
+    w_all,
+    gain_rows,
+    at_out,
+    bt_out,
+    et_out,
+    qh,
+    kh,
+    vh,
+    lse,
+    ob,
+    x2,
+    gate,
+    up,
+    hidden,
+    out_part,
+    a_buf,
+    gw,
+    wbuf,
+    kvx,
+    oh,
+    xs,
+    xr,
+    acc,
+    z_send,
+    z_recv,
+    y_send,
+    y_recv,
+    c_send,
+    c_recv,
+    kv_send,
+    kv_recv,
+    x_send,
+    x_recv,
+    own_sem,
+    load_sem,
+):
+    me = Place()
+    f, y, k = me.f, me.y, me.k
+    units = packed.shape[0]
+    groups = gate.shape[0]
+    scale = 1.0 / math.sqrt(HD)
+
+    own = pltpu.make_async_copy(packed, w_all.at[:, f, y, k], own_sem.at[0])
+    own.start()
+    own_gain = pltpu.make_async_copy(gains, gw.at[0, f, y, k], own_sem.at[1])
+    own_gain.start()
+    me.barrier()
+
+    def z_start(src, buf, j, s):
+        for i, device in enumerate((me.near, me.mid)):
+            remote(src, buf.at[j, f, y, k], z_send.at[s, i], z_recv.at[s], device).start()
+
+    def hand_on(buf, j, s):
+        part = buf.at[j, pl.ds(2 - 2 * me.half, 2), y, k]
+        return remote(part, part, z_send.at[s, 2], z_recv.at[s], me.near)
+
+    def y_copy(buf, j, s):
+        part = buf.at[j, :, y, k]
+        return remote(part, part, y_send.at[s], y_recv.at[s], me.ypeer)
+
+    def core_copy(buf, j, s):
+        part = buf.at[j, :, :, k]
+        return remote(part, part, c_send.at[s], c_recv.at[s], me.sib)
+
+    def stage_y(buf, j, s):
+        three = buf.at[j, pl.ds(0, 3), y, k]
+        remote(three, three, z_send.at[s, 0], z_recv.at[s], me.near).wait_recv()
+
+        @pl.when(me.inner)
+        def _():
+            hand_on(buf, j, s).start()
+
+        y_copy(buf, j, s).start()
+
+    def stage_core(buf, j, s):
+        y_copy(buf, j, s).wait_recv()
+        core_copy(buf, j, s).start()
+
+    def stage_done(buf, j, s):
+        core_copy(buf, j, s).wait_recv()
+
+    def sends_done(buf, j, s):
+        for i, device in enumerate((me.near, me.mid)):
+            remote(buf.at[j, f, y, k], buf.at[j, f, y, k], z_send.at[s, i], z_recv.at[s], device).wait_send()
+
+        @pl.when(me.inner)
+        def _():
+            hand_on(buf, j, s).wait_send()
+
+        y_copy(buf, j, s).wait_send()
+        core_copy(buf, j, s).wait_send()
+
+    ahead = 4
+
+    def step(u):
+        def guarded(low_ok, high_ok, act):
+            if isinstance(u, int):
+                if low_ok and high_ok:
+                    act()
+            else:
+                pl.when(high_ok)(act)
+
+        guarded(True, u + ahead < units, lambda: z_start(packed.at[u + ahead], w_all, u + ahead, u + ahead))
+        guarded(True, u < units, lambda: stage_y(w_all, u, u))
+        guarded(not isinstance(u, int) or u >= 1, u - 1 < units, lambda: stage_core(w_all, u - 1, u - 1))
+        guarded(not isinstance(u, int) or u >= 2, u - 2 < units, lambda: stage_done(w_all, u - 2, u - 2))
+
+    def load(u, slot, side):
+        return pltpu.make_async_copy(
+            w_all.at[u],
+            wbuf.at[slot, :, :, :, :, pl.ds(side * UNIT, UNIT)],
+            load_sem.at[slot, side],
+        )
+
+    z_start(gains, gw, 0, units)
+    for u in range(ahead):
+        z_start(packed.at[u], w_all, u, u)
+    own.wait()
+    own_gain.wait()
+    stage_y(gw, 0, units)
+    transpose_into(et_out, cot)
+    stage_core(gw, 0, units)
+    stage_done(gw, 0, units)
+    gain_rows[...] = gw[0].reshape(WIDE, 128).astype(F32).T[:8, :]
+    step(0)
+
+    @pl.loop(0, ROWS // 64)
+    def _(i):
+        rows = pl.ds(pl.multiple_of(i * 64, 64), 64)
+        x = tokens[rows, :].astype(F32)
+        r = lax.rsqrt(jnp.mean(x * x, axis=-1, keepdims=True) + epsilon)
+        a_buf[rows, :] = (x * r * gain_rows[0:1, :]).astype(BF16)
+
+    step(1)
+    transpose_into(at_out, a_buf)
+    step(2)
+    load(0, 0, 0).start()
+    step(3)
+    load(1, 0, 1).start()
+    load(0, 0, 0).wait()
+    for s in range(2):
+        rows = pl.ds(s * SPAN, SPAN)
+        key = turn(dot_nn(a_buf[rows, :], weight(wbuf, 0, 0, UNIT)), cosine[...], sine[...])
+        kvx[y, k, rows, 0:UNIT] = key.astype(BF16)
+    load(1, 0, 1).wait()
+    kvx[y, k, :, UNIT:] = dot_nn(a_buf[...], weight(wbuf, 0, UNIT, 2 * UNIT)).astype(BF16)
+
+    def kv_copy(stage):
+        part = kvx.at[y, k] if stage == 0 else kvx.at[:, k]
+        return remote(part, part, kv_send.at[stage], kv_recv.at[stage], me.ypeer if stage == 0 else me.sib)
+
+    kv_copy(0).start()
+    step(4)
+    load(2, 1, 0).start()
+    step(5)
+    load(3, 1, 1).start()
+    load(2, 1, 0).wait()
+    load(3, 1, 1).wait()
+    for side in range(2):
+        for s in range(2):
+            rows = pl.ds(s * SPAN, SPAN)
+            columns = slice(side * UNIT, (side + 1) * UNIT)
+            query = dot_nn(a_buf[rows, :], weight(wbuf, 1, side * UNIT, (side + 1) * UNIT))
+            query = turn(query, cosine[...], sine[...])
+            for i, head in enumerate(unpack_heads(query)):
+                qh[s * 8 + side * 4 + i] = head.astype(BF16)
+    kv_copy(0).wait_recv()
+    kv_copy(1).start()
+    step(6)
+    load(4, 0, 0).start()
+    step(7)
+    load(5, 0, 1).start()
+    kv_copy(1).wait_recv()
+
+    @pl.loop(0, 8)
+    def _(i):
+        s, c = lax.div(i, 4), lax.rem(i, 4)
+        block = kvx[lax.div(c, 2), lax.rem(c, 2), pl.ds(pl.multiple_of(s * SPAN, SPAN), SPAN), :]
+        at = pl.ds(pl.multiple_of(c * SPAN, SPAN), SPAN)
+        for g, head in enumerate(unpack_heads(block[:, :UNIT].astype(F32))):
+            kh[s * 4 + g, at, :] = head.astype(BF16)
+        for g, head in enumerate(unpack_heads(block[:, UNIT:].astype(F32))):
+            vh[s * 4 + g, at, :] = head.astype(BF16)
+
+    def attend(i):
+        s, h = lax.div(i, 8), lax.rem(i, 8)
+        g = s * 4 + lax.div(h, 2)
+        scores = dot_nt(kh[g], qh[i]) * scale
+        scores = jnp.where(allowed_keys(low[s], high[...]), scores, negative)
+        top = jnp.max(scores, axis=0, keepdims=True)
+        p = jnp.exp(scores - top)
+        total = jnp.sum(p, axis=0, keepdims=True)
+        lse[i] = jnp.broadcast_to(top + jnp.log(total), (8, SPAN))
+        oh[h] = (dot_tn(vh[g], p.astype(BF16)) / total).T
+
+    def gather_heads(s):
+        for side in range(2):
+            ob[s * SPAN : (s + 1) * SPAN, side * UNIT : (side + 1) * UNIT] = pack_heads(
+                [oh[side * 4 + i] for i in range(4)]
+            ).astype(BF16)
+
+    pl.loop(0, 8)(attend)
+    gather_heads(0)
+    step(8)
+    pl.loop(8, 16)(attend)
+    gather_heads(1)
+    load(4, 0, 0).wait()
+    load(5, 0, 1).wait()
+
+    def x_copy(r):
+        rows = pl.ds(pl.multiple_of(r * 128, 128), 128)
+        return remote(xs.at[rows], xr.at[rows], x_send.at[r], x_recv.at[r], me.xpeer)
+
+    for r in range(4):
+        rows = slice(r * 128, (r + 1) * 128)
+        xs[rows, :] = dot_nt(ob[rows, :], weight(wbuf, 0, 0, 2 * UNIT)).astype(BF16)
+        x_copy(r).start()
+    for u in range(9, 13):
+        step(u)
+
+    @pl.loop(0, 4)
+    def _(r):
+        x_copy(r).wait()
+        rows = pl.ds(pl.multiple_of(r * 128, 128), 128)
+        x = tokens[rows, :].astype(F32) + (xs[rows, :].astype(F32) + xr[rows, :].astype(F32))
+        x2[rows, :] = x
+        r2 = lax.rsqrt(jnp.mean(x * x, axis=-1, keepdims=True) + epsilon)
+        a_buf[rows, :] = (x * r2 * gain_rows[1:2, :]).astype(BF16)
+
+    acc[...] = jnp.zeros_like(acc)
+
+    def feed(n, slot):
+        for side in range(2):
+            load(6 + 2 * n + side, slot, side).wait()
+        gate_n = dot_nn(a_buf[...], weight(wbuf, slot, 0, 256))
+        up_n = dot_nn(a_buf[...], weight(wbuf, slot, 256, 512))
+        hidden_n = (gate_n * jax.nn.sigmoid(gate_n) * up_n).astype(BF16)
+        gate[n] = gate_n.astype(BF16)
+        up[n] = up_n.astype(BF16)
+        hidden[n] = hidden_n
+        acc[...] += dot_nt(hidden_n, weight(wbuf, slot, 512, 768))
+
+    @pl.loop(0, groups)
+    def _(n):
+        first = 6 + 2 * n
+        slot = lax.rem(n, 2)
+
+        @pl.when(n >= 3)
+        def _():
+            step(first + 2)
+            step(first + 3)
+
+        for side in range(2):
+            load(first + side, slot, side).start()
+
+        @pl.when(n == 0)
+        def _():
+            transpose_into(bt_out, a_buf)
+            step(13)
+
+        feed(n, slot)
+
+    out_part[...] = acc[...].astype(BF16)
+    kv_copy(0).wait_send()
+    kv_copy(1).wait_send()
+    sends_done(gw, 0, units)
+
+    @pl.loop(0, units)
+    def _(u):
+        sends_done(w_all, u, u)
+
+
+def rope_inputs(row_count):
+    positions = lax.axis_index("ctx") * row_count + jnp.arange(row_count, dtype=jnp.int32)
+    cosine_table, sine_table = rope_tables(positions)
+    cosine = jnp.tile(cosine_table, (1, 2 * UNIT // HD))
+    sine = jnp.tile(jnp.concatenate([-sine_table, sine_table], axis=1), (1, UNIT // HD))
+    return positions, cosine, sine
+
+
+def pack_weights(w_query, w_key, w_value, w_out, w_gate, w_up, w_down):
+    depth = w_query.shape[0]
+    groups = w_gate.shape[1] // 256
+    fed = jnp.concatenate(
+        [part.reshape(depth, groups, 256) for part in (w_gate, w_up, w_down.T)], axis=2
+    ).reshape(depth, groups * 2 * UNIT)
+    flat = jnp.concatenate([w_key, w_value, w_query, w_out.T, fed], axis=1)
+    return jnp.transpose(flat.reshape(depth, flat.shape[1] // UNIT, UNIT), (1, 0, 2))
+
+
+def pack_gains(gain_attn, gain_mlp):
+    return jnp.pad(jnp.stack([gain_attn, gain_mlp], axis=1), ((0, 0), (0, 126)))
+
+
+def vmem(shape, dtype):
+    return pltpu.VMEM(shape, dtype)
+
+
+def call_forward(packed, gains, tokens, cot, cosine, sine, low, high):
+    units, depth = packed.shape[0], packed.shape[1]
+    groups = (units - 6) // 2
+    struct = jax.ShapeDtypeStruct
+    any_spec = pl.BlockSpec(memory_space=pl.ANY)
+    vmem_spec = pl.BlockSpec(memory_space=pltpu.VMEM)
+    block = (4, 2, 2, depth)
+    dma = pltpu.SemaphoreType.DMA
+    return pl.pallas_call(
+        forward_kernel,
+        out_shape=(
+            struct((units,) + block + (UNIT,), BF16),
+            struct((8, WIDE), F32),
+            struct((WIDE, ROWS), BF16),
+            struct((WIDE, ROWS), BF16),
+            struct((WIDE, ROWS), BF16),
+            struct((16, SPAN, 128), BF16),
+            struct((8, 4 * SPAN, 128), BF16),
+            struct((8, 4 * SPAN, 128), BF16),
+            struct((16, 8, SPAN), F32),
+            struct((ROWS, 2 * UNIT), BF16),
+            struct((ROWS, WIDE), F32),
+            struct((groups, ROWS, 256), BF16),
+            struct((groups, ROWS, 256), BF16),
+            struct((groups, ROWS, 256), BF16),
+            struct((ROWS, WIDE), BF16),
+        ),
+        in_specs=[any_spec, any_spec] + [vmem_spec] * 6,
+        out_specs=(any_spec,) + (vmem_spec,) * 14,
+        scratch_shapes=[
+            vmem((ROWS, WIDE), BF16),
+            vmem((1,) + block + (128,), BF16),
+            vmem((2,) + block + (2 * UNIT,), BF16),
+            vmem((2, 2, ROWS, 2 * UNIT), BF16),
+            vmem((8, SPAN, 128), F32),
+            vmem((ROWS, WIDE), BF16),
+            vmem((ROWS, WIDE), BF16),
+            vmem((ROWS, WIDE), F32),
+            dma((units + 1, 3)),
+            dma((units + 1,)),
+            dma((units + 1,)),
+            dma((units + 1,)),
+            dma((units + 1,)),
+            dma((units + 1,)),
+            dma((2,)),
+            dma((2,)),
+            dma((4,)),
+            dma((4,)),
+            dma((2,)),
+            dma((2, 2)),
+        ],
+        compiler_params=pltpu.CompilerParams(
+            collective_id=1, has_side_effects=True, vmem_limit_bytes=60 << 20
+        ),
+        name="forward",
+    )(packed, gains, tokens, cot, cosine, sine, low, high)
+
+
+RING = 5
+
+
+def backward_kernel(
+    w_all,
+    gain_rows,
+    tokens,
+    cot,
+    at_in,
+    bt_in,
+    et_in,
+    gate,
+    up,
+    hidden,
+    out_part,
+    qh,
+    kh,
+    vh,
+    lse,
+    ob,
+    x2,
+    cosine,
+    sine,
+    low,
+    high,
+    output,
+    grad_tokens,
+    grads,
+    gain_grads,
+    eb,
+    et,
+    bt,
+    dxt,
+    dg,
+    du,
+    gu,
+    hbuf,
+    wbuf,
+    part,
+    r1,
+    r2,
+    r3,
+    acc,
+    xs,
+    xr,
+    doh,
+    dqh,
+    dkh,
+    dvh,
+    dkv,
+    rc,
+    ry,
+    dqb,
+    dkvb,
+    gacc,
+    gp,
+    g1,
+    g2,
+    g3,
+    gs,
+    c_send,
+    c_recv,
+    y_send,
+    y_recv,
+    za_send,
+    za_recv,
+    zb_send,
+    zb_recv,
+    c_cred,
+    y_cred,
+    z_cred,
+    x_send,
+    x_recv,
+    x_cred,
+    kv_send,
+    kv_recv,
+    g_send,
+    g_recv,
+    load_sem,
+    w_sem,
+    h_sem,
+    gout,
+    out_sem,
+):
+    me = Place()
+    f, y, k = me.f, me.y, me.k
+    units = grads.shape[0]
+    groups = gate.shape[0]
+    scale = 1.0 / math.sqrt(HD)
+
+    def local(src, dst, i):
+        return pltpu.make_async_copy(src, dst, load_sem.at[i])
+
+    def load(u, slot, side):
+        return pltpu.make_async_copy(
+            w_all.at[u],
+            wbuf.at[slot, :, :, :, :, pl.ds(side * UNIT, UNIT)],
+            w_sem.at[slot, side],
+        )
+
+    def load_pair(u, slot):
+        for side in range(2):
+            load(u + side, slot, side).start()
+
+    def wait_pair(u, slot):
+        for side in range(2):
+            load(u + side, slot, side).wait()
+
+    def gu_copies(n, slot):
+        return [
+            pltpu.make_async_copy(src.at[n], gu.at[slot, i], h_sem.at[slot, i])
+            for i, src in enumerate((gate, up))
+        ]
+
+    def h_copy(n, slot):
+        return pltpu.make_async_copy(hidden.at[n], hbuf.at[slot], h_sem.at[slot, 2])
+
+    load_pair(6, 0)
+    for copy in gu_copies(0, 0):
+        copy.start()
+    local(cot, eb, 0).start()
+    local(bt_in, bt, 1).start()
+    local(et_in, et, 2).start()
+    h_copy(0, 0).start()
+    me.barrier()
+
+    class Unit:
+        def __init__(self, r):
+            self.r = r
+            self.ring = True
+            self.s = lax.rem(r, RING)
+            self.first = r < RING
+            self.last = r + RING >= units
+            slot = lax.rem(lax.div(r, 2), 2)
+            columns = pl.ds(pl.multiple_of(lax.rem(r, 2) * UNIT, 128), UNIT)
+            self.other = part.at[slot, :, :, me.ok, :, columns]
+            self.mine = part.at[slot, :, :, k, :, columns]
+            self.r1, self.r2, self.r3 = r1.at[self.s], r2.at[self.s], r3.at[self.s]
+
+    class GainUnit:
+        def __init__(self):
+            self.r = units
+            self.ring = False
+            self.other = gp.at[:, :, me.ok]
+            self.mine = gp.at[:, :, k]
+            self.r1, self.r2, self.r3 = g1, g2, g3
+
+    def credit(unit, sem):
+        if unit.ring:
+
+            @pl.when(jnp.logical_not(unit.first))
+            def _():
+                pl.semaphore_wait(sem, 1)
+
+    def give(unit, sem, device):
+        if unit.ring:
+
+            @pl.when(jnp.logical_not(unit.last))
+            def _():
+                pl.semaphore_signal(sem, inc=1, device_id=device, device_id_type=MESH)
+
+    def core_copy(unit):
+        return remote(unit.other, unit.r1, c_send.at[unit.r], c_recv.at[unit.r], me.sib)
+
+    def y_copy(unit):
+        return remote(unit.r1.at[:, me.oy], unit.r2, y_send.at[unit.r], y_recv.at[unit.r], me.ypeer)
+
+    def za_copy(unit):
+        return remote(
+            unit.r2.at[pl.ds(1 - me.half, 3)],
+            unit.r3.at[pl.ds(0, 3)],
+            za_send.at[unit.r],
+            za_recv.at[unit.r],
+            me.near,
+        )
+
+    def zb_copy(unit, i):
+        owner, at, device = (
+            (me.near_f, 0, me.near),
+            (me.mid_f, 3, me.mid),
+            (me.far_f, 1, me.far),
+        )[i]
+        return remote(
+            unit.r2.at[owner],
+            unit.r3.at[at],
+            zb_send.at[unit.r, i],
+            zb_recv.at[unit.r, min(i, 1)],
+            device,
+        )
+
+    def stage_core(unit):
+        credit(unit, c_cred)
+        core_copy(unit).start()
+
+    def stage_y(unit):
+        core_copy(unit).wait_recv()
+        unit.r1[...] = unit.r1[...] + unit.mine[...]
+        core_copy(unit).wait_send()
+        credit(unit, y_cred)
+        y_copy(unit).start()
+
+    def stage_z(unit):
+        y_copy(unit).wait_recv()
+        unit.r2[...] = unit.r2[...] + unit.r1[:, y]
+        y_copy(unit).wait_send()
+        give(unit, c_cred, me.sib)
+
+        @pl.when(me.edge)
+        def _():
+            credit(unit, z_cred.at[0])
+            za_copy(unit).start()
+
+    def stage_zb(unit):
+        @pl.when(me.inner)
+        def _():
+            za_copy(unit).wait_recv()
+            for owner in (me.mid_f, me.far_f):
+                unit.r2[owner] = unit.r2[owner] + unit.r3[owner - (1 - me.half)]
+            for i in range(3):
+                credit(unit, z_cred.at[i])
+                zb_copy(unit, i).start()
+
+    def stage_end(unit, store):
+        zb_copy(unit, 1).wait_recv()
+
+        @pl.when(me.edge)
+        def _():
+            zb_copy(unit, 0).wait_recv()
+
+        one = jnp.where(me.edge, 0, f - (1 - me.half))
+        two = jnp.where(me.edge, 1, 3)
+        store(unit.r2[f].astype(F32) + unit.r3[one].astype(F32) + unit.r3[two].astype(F32))
+
+        @pl.when(me.edge)
+        def _():
+            za_copy(unit).wait_send()
+            give(unit, z_cred.at[0], me.near)
+            give(unit, z_cred.at[2], me.mid)
+
+        @pl.when(me.inner)
+        def _():
+            for i in range(3):
+                zb_copy(unit, i).wait_send()
+            give(unit, z_cred.at[0], me.near)
+            give(unit, z_cred.at[1], me.mid)
+
+        give(unit, y_cred, me.ypeer)
+
+    def out_copy(i):
+        slot = lax.rem(i, 2)
+        return pltpu.make_async_copy(gout.at[slot], grads.at[i], out_sem.at[slot])
+
+    def step(r):
+        def guarded(lag, act):
+            i = r - lag
+            if isinstance(r, int):
+                if 0 <= i < units:
+                    act(i)
+            else:
+                pl.when((i >= 0) & (i < units))(lambda: act(i))
+
+        def end(i):
+            slot = lax.rem(i, 2)
+
+            def store(total):
+                @pl.when(i >= 2)
+                def _():
+                    out_copy(i - 2).wait()
+
+                gout[slot] = total
+                out_copy(i).start()
+
+            stage_end(Unit(i), store)
+
+        guarded(0, lambda i: stage_core(Unit(i)))
+        guarded(1, lambda i: stage_y(Unit(i)))
+        guarded(2, lambda i: stage_z(Unit(i)))
+        guarded(3, lambda i: stage_zb(Unit(i)))
+        guarded(4, end)
+
+    depth = r2.shape[2]
+
+    def put(pair, columns, value):
+        part[lax.rem(pair, 2), :, :, :, :, columns] = value.astype(BF16).reshape(4, 2, 2, depth, 256)
+
+    def feed_grads(n, pair):
+        slot = lax.rem(n, 2)
+        h_copy(n, slot).wait()
+        put(pair, slice(0, 256), dot_nn(bt[...], dg[n]))
+        put(pair, slice(256, 512), dot_nn(bt[...], du[n]))
+        put(pair, slice(512, 768), dot_nn(et[...], hbuf[slot]))
+
+        @pl.when(n + 1 < groups)
+        def _():
+            h_copy(n + 1, 1 - slot).start()
+
+    local(cot, eb, 0).wait()
+    local(bt_in, bt, 1).wait()
+    local(et_in, et, 2).wait()
+    acc[...] = jnp.zeros_like(acc)
+
+    @pl.loop(0, groups)
+    def _(n):
+        slot = lax.rem(n, 2)
+
+        @pl.when(n + 1 < groups)
+        def _():
+            load_pair(6 + 2 * (n + 1), 1 - slot)
+            for copy in gu_copies(n + 1, 1 - slot):
+                copy.start()
+
+        wait_pair(6 + 2 * n, slot)
+        for copy in gu_copies(n, slot):
+            copy.wait()
+        dh = dot_nn(eb[...], weight(wbuf, slot, 512, 768))
+        g = gu[slot, 0].astype(F32)
+        u = gu[slot, 1].astype(F32)
+        sg = jax.nn.sigmoid(g)
+        dg[n] = (dh * u * sg * (1.0 + g * (1.0 - sg))).astype(BF16)
+        du[n] = (dh * g * sg).astype(BF16)
+
+        @pl.loop(0, 4)
+        def _(r):
+            rows = pl.ds(pl.multiple_of(r * 128, 128), 128)
+            acc[rows, :] += dot_nt(dg[n, rows, :], weight(wbuf, slot, 0, 256)) + dot_nt(
+                du[n, rows, :], weight(wbuf, slot, 256, 512)
+            )
+
+        @pl.when((n == 0) | (n == 4))
+        def _():
+            pair = lax.div(n, 4)
+            feed_grads(pair, pair)
+            step(2 * pair)
+            step(2 * pair + 1)
+
+    load_pair(4, 0)
+
+    def x_copy(e, r, src):
+        rows = pl.ds(r * 128, 128)
+        return remote(src.at[rows], xr.at[rows], x_send.at[e, r], x_recv.at[e, r], me.xpeer)
+
+    for r in range(4):
+        rows = slice(r * 128, (r + 1) * 128)
+        xs[rows, :] = acc[rows, :].astype(BF16)
+        x_copy(0, r, xs).start()
+
+    @pl.loop(2, 4)
+    def _(n):
+        feed_grads(n, n)
+        step(2 * n)
+        step(2 * n + 1)
+
+    gacc[...] = jnp.zeros_like(gacc)
+    for r in range(4):
+        rows = slice(r * 128, (r + 1) * 128)
+        x_copy(0, r, xs).wait()
+        own = xs[rows, :].astype(F32)
+        db = own + xr[rows, :].astype(F32)
+        x = x2[rows, :]
+        r2_rows = lax.rsqrt(jnp.mean(x * x, axis=-1, keepdims=True) + epsilon)
+        n2 = x * r2_rows
+        gacc[1:2, :] += jnp.sum(own * n2, axis=0, keepdims=True)
+        scaled = db * gain_rows[1:2, :]
+        dx2 = eb[rows, :].astype(F32) + r2_rows * (
+            scaled - n2 * jnp.mean(scaled * n2, axis=-1, keepdims=True)
+        )
+        acc[rows, :] = dx2
+        eb[rows, :] = dx2.astype(BF16)
+
+    def give_x():
+        pl.semaphore_signal(x_cred, inc=1, device_id=me.xpeer, device_id_type=MESH)
+
+    give_x()
+    local(out_part, xs, 0).start()
+    pl.semaphore_wait(x_cred, 1)
+    for r in range(4):
+        x_copy(1, r, out_part).start()
+
+    transpose_into(dxt, eb)
+    for i in range(3):
+        put(4, slice(i * 256, (i + 1) * 256), dot_nn(dxt[...], ob[:, i * 256 : (i + 1) * 256]))
+    step(8)
+    wait_pair(4, 0)
+    for s in range(2):
+        rows = slice(s * SPAN, (s + 1) * SPAN)
+        for side in range(2):
+            columns = (side * UNIT, (side + 1) * UNIT)
+            mixed = dot_nn(eb[rows, :], weight(wbuf, 0, *columns)).astype(BF16).astype(F32)
+            for i, head in enumerate(unpack_heads(mixed)):
+                doh[s * 8 + side * 4 + i] = head.astype(BF16)
+    step(9)
+    load_pair(2, 0)
+    load_pair(0, 1)
+    local(tokens, eb, 1).start()
+
+    def attend_back(i):
+        s, g = lax.div(i, 4), lax.rem(i, 4)
+        mask = allowed_keys(low[s], high[...])
+        dk = jnp.zeros((4 * SPAN, 128), F32)
+        dv = jnp.zeros((4 * SPAN, 128), F32)
+        for hh in range(2):
+            h = s * 8 + 2 * g + hh
+            scores = jnp.where(mask, dot_nt(kh[i], qh[h]) * scale, negative)
+            p = jnp.exp(scores - lse[h][0:1, :])
+            dp = dot_nt(vh[i], doh[h])
+            delta = jnp.sum(p * dp, axis=0, keepdims=True)
+            ds = (p * (dp - delta) * scale).astype(BF16)
+            dv += dot_nn(p.astype(BF16), doh[h])
+            dk += dot_nn(ds, qh[h])
+            dqh[2 * g + hh] = dot_tn(kh[i], ds).T
+        dkh[g] = dk.astype(BF16)
+        dvh[g] = dv.astype(BF16)
+
+    def kv_core(s):
+        return remote(dkv.at[s, :, me.ok], rc.at[s], kv_send.at[0, s], kv_recv.at[0, s], me.sib)
+
+    def kv_y(s):
+        return remote(rc.at[s, me.oy], ry.at[s], kv_send.at[1, s], kv_recv.at[1, s], me.ypeer)
+
+    @pl.loop(0, 4)
+    def _(i):
+        attend_back(2 * i)
+        attend_back(2 * i + 1)
+        feed_grads(4 + i, 5 + i)
+        step(10 + 2 * i)
+
+        @pl.when(lax.rem(i, 2) == 1)
+        def _():
+            s = lax.div(i, 2)
+            for c in range(4):
+                rows = slice(c * SPAN, (c + 1) * SPAN)
+                for j, heads in enumerate((dkh, dvh)):
+                    dkv[s, c // 2, c % 2, :, j * UNIT : (j + 1) * UNIT] = pack_heads(
+                        [heads[g, rows, :].astype(F32) for g in range(4)]
+                    ).astype(BF16)
+            kv_core(s).start()
+            rows = pl.ds(pl.multiple_of(s * SPAN, SPAN), SPAN)
+            for side in range(2):
+                dq = turn(pack_heads([dqh[side * 4 + j] for j in range(4)]), cosine[...], -sine[...])
+                dqb[rows, side * UNIT : (side + 1) * UNIT] = dq.astype(BF16)
+
+        step(11 + 2 * i)
+
+    local(at_in, bt, 2).start()
+    for s in range(2):
+        kv_core(s).wait_recv()
+        rc[s] = rc[s] + dkv[s, :, k]
+        kv_y(s).start()
+    local(at_in, bt, 2).wait()
+    for i in range(3):
+        put(9, slice(i * 256, (i + 1) * 256), dot_nn(bt[...], dqb[:, i * 256 : (i + 1) * 256]))
+    step(18)
+
+    local(out_part, xs, 0).wait()
+    for r in range(4):
+        rows = slice(r * 128, (r + 1) * 128)
+        x_copy(1, r, out_part).wait()
+        xs[rows, :] = (x2[rows, :] + (xs[rows, :].astype(F32) + xr[rows, :].astype(F32))).astype(BF16)
+    give_x()
+    local(xs, output, 0).start()
+    step(19)
+    wait_pair(2, 0)
+    wait_pair(0, 1)
+    local(tokens, eb, 1).wait()
+    for s in range(2):
+        rows = slice(s * SPAN, (s + 1) * SPAN)
+        kv_y(s).wait_recv()
+        total = rc[s, y].astype(F32) + ry[s].astype(F32)
+        dkvb[rows, :UNIT] = turn(total[:, :UNIT], cosine[...], -sine[...]).astype(BF16)
+        dkvb[rows, UNIT:] = total[:, UNIT:].astype(BF16)
+    for i in range(3):
+        put(10, slice(i * 256, (i + 1) * 256), dot_nn(bt[...], dkvb[:, i * 256 : (i + 1) * 256]))
+    step(20)
+    local(xs, output, 0).wait()
+    pl.semaphore_wait(x_cred, 1)
+
+    def first_norm(rows):
+        x = eb[rows, :].astype(F32)
+        r1_rows = lax.rsqrt(jnp.mean(x * x, axis=-1, keepdims=True) + epsilon)
+        return r1_rows, x * r1_rows
+
+    for r in range(4):
+        rows = slice(r * 128, (r + 1) * 128)
+        da = dot_nt(dqb[rows, :], weight(wbuf, 0, 0, 768)) + dot_nt(dkvb[rows, :], weight(wbuf, 1, 0, 768))
+        xs[rows, :] = da.astype(BF16)
+        x_copy(2, r, xs).start()
+        gacc[0:1, :] += jnp.sum(xs[rows, :].astype(F32) * first_norm(rows)[1], axis=0, keepdims=True)
+    step(21)
+    gain_columns = jnp.concatenate([gacc[...], jnp.zeros((120, WIDE), F32)], axis=0).T
+    gp[...] = gain_columns.astype(BF16).reshape(4, 2, 2, depth, 128)
+    gain = GainUnit()
+    stage_core(gain)
+    step(22)
+    stage_y(gain)
+    step(23)
+    stage_z(gain)
+
+    for r in range(4):
+        rows = slice(r * 128, (r + 1) * 128)
+        x_copy(2, r, xs).wait()
+        da = xs[rows, :].astype(F32) + xr[rows, :].astype(F32)
+        r1_rows, n1 = first_norm(rows)
+        scaled = da * gain_rows[0:1, :]
+        acc[rows, :] += r1_rows * (scaled - n1 * jnp.mean(scaled * n1, axis=-1, keepdims=True))
+    local(acc, grad_tokens, 0).start()
+    stage_zb(gain)
+    step(24)
+
+    def store_gain(total):
+        gs[0] = total
+
+    stage_end(gain, store_gain)
+    pair_copy = remote(gs.at[0], gs.at[1], g_send.at[0], g_recv.at[0], me.xpeer)
+    pair_copy.start()
+    step(25)
+    pair_copy.wait()
+    out_copy(units - 2).wait()
+    out_copy(units - 1).wait()
+    gain_grads[...] = gs[0] + gs[1]
+    for s in range(2):
+        kv_core(s).wait_send()
+        kv_y(s).wait_send()
+    local(acc, grad_tokens, 0).wait()
+
+
+def call_backward(w_all, gain_rows, tokens, cot, at, bt, et, gate, up, hidden, out_part, *rest):
+    units, depth = w_all.shape[0], w_all.shape[4]
+    groups = gate.shape[0]
+    struct = jax.ShapeDtypeStruct
+    any_spec = pl.BlockSpec(memory_space=pl.ANY)
+    vmem_spec = pl.BlockSpec(memory_space=pltpu.VMEM)
+    dma = pltpu.SemaphoreType.DMA
+    regular = pltpu.SemaphoreType.REGULAR
+    return pl.pallas_call(
+        backward_kernel,
+        out_shape=(
+            struct((ROWS, WIDE), BF16),
+            struct((ROWS, WIDE), F32),
+            struct((units, depth, UNIT), F32),
+            struct((depth, 128), F32),
+        ),
+        in_specs=[any_spec, vmem_spec] + [any_spec] * 9 + [vmem_spec] * 10,
+        out_specs=(any_spec, any_spec, any_spec, vmem_spec),
+        scratch_shapes=[
+            vmem((ROWS, WIDE), BF16),
+            vmem((WIDE, ROWS), BF16),
+            vmem((WIDE, ROWS), BF16),
+            vmem((WIDE, ROWS), BF16),
+            vmem((groups, ROWS, 256), BF16),
+            vmem((groups, ROWS, 256), BF16),
+            vmem((2, 2, ROWS, 256), BF16),
+            vmem((2, ROWS, 256), BF16),
+            vmem((2, 4, 2, 2, depth, 2 * UNIT), BF16),
+            vmem((2, 4, 2, 2, depth, 2 * UNIT), BF16),
+            vmem((RING, 4, 2, depth, UNIT), BF16),
+            vmem((RING, 4, depth, UNIT), BF16),
+            vmem((RING, 4, depth, UNIT), BF16),
+            vmem((ROWS, WIDE), F32),
+            vmem((ROWS, WIDE), BF16),
+            vmem((ROWS, WIDE), BF16),
+            vmem((16, SPAN, 128), BF16),
+            vmem((8, SPAN, 128), F32),
+            vmem((4, 4 * SPAN, 128), BF16),
+            vmem((4, 4 * SPAN, 128), BF16),
+            vmem((2, 2, 2, SPAN, 2 * UNIT), BF16),
+            vmem((2, 2, SPAN, 2 * UNIT), BF16),
+            vmem((2, SPAN, 2 * UNIT), BF16),
+            vmem((ROWS, 2 * UNIT), BF16),
+            vmem((ROWS, 2 * UNIT), BF16),
+            vmem((8, WIDE), F32),
+            vmem((4, 2, 2, depth, 128), BF16),
+            vmem((4, 2, depth, 128), BF16),
+            vmem((4, depth, 128), BF16),
+            vmem((4, depth, 128), BF16),
+            vmem((2, depth, 128), F32),
+            dma((units + 1,)),
+            dma((units + 1,)),
+            dma((units + 1,)),
+            dma((units + 1,)),
+            dma((units + 1,)),
+            dma((units + 1,)),
+            dma((units + 1, 3)),
+            dma((units + 1, 2)),
+            regular,
+            regular,
+            regular((3,)),
+            dma((3, 4)),
+            dma((3, 4)),
+            regular,
+            dma((2, 2)),
+            dma((2, 2)),
+            dma((1,)),
+            dma((1,)),
+            dma((3,)),
+            dma((2, 2)),
+            dma((2, 3)),
+            vmem((2, depth, UNIT), F32),
+            dma((2,)),
+        ],
+        compiler_params=pltpu.CompilerParams(
+            collective_id=2, has_side_effects=True, vmem_limit_bytes=64 << 20
+        ),
+        name="backward",
+    )(w_all, gain_rows, tokens, cot, at, bt, et, gate, up, hidden, out_part, *rest)
+
+
+def fast_body(
+    tokens,
+    segments,
+    cotangent,
+    gain_attn,
+    w_query,
+    w_key,
+    w_value,
+    w_out,
+    gain_mlp,
+    w_gate,
+    w_up,
+    w_down,
+):
+    positions, cosine, sine = rope_inputs(SPAN)
+    mine = lax.dynamic_slice_in_dim(segments, positions[0], SPAN, 1)
+    low = jnp.sum((segments[:, None, :] < mine[:, :, None]).astype(jnp.int32), axis=-1)[:, None, :]
+    high = positions[None, :]
+    packed = pack_weights(w_query, w_key, w_value, w_out, w_gate, w_up, w_down)
+    gains = pack_gains(gain_attn, gain_mlp)
+    flat_tokens = tokens.reshape(ROWS, WIDE)
+    flat_cot = cotangent.reshape(ROWS, WIDE)
+    (
+        w_all,
+        gain_rows,
+        at,
+        bt,
+        et,
+        qh,
+        kh,
+        vh,
+        lse,
+        ob,
+        x2,
+        gate,
+        up,
+        hidden,
+        out_part,
+    ) = call_forward(packed, gains, flat_tokens, flat_cot, cosine, sine, low, high)
+    output, grad_tokens, grads, gain_grads = call_backward(
+        w_all,
+        gain_rows,
+        flat_tokens,
+        flat_cot,
+        at,
+        bt,
+        et,
+        gate,
+        up,
+        hidden,
+        out_part,
+        qh,
+        kh,
+        vh,
+        lse,
+        ob,
+        x2,
+        cosine,
+        sine,
+        low,
+        high,
+    )
+
+    def span(lo, hi):
+        return jnp.concatenate([grads[i] for i in range(lo, hi)], axis=1)
+
+    fed = [span(2 * i, 2 * i + 2) for i in (0, 1, 2, 3, 5, 6, 7, 8)]
+    gate_grad, up_grad, down_grad = (
+        jnp.concatenate([group[:, i * 256 : (i + 1) * 256] for group in fed], axis=1) for i in range(3)
+    )
+    return (
+        output.reshape(tokens.shape),
+        grad_tokens.reshape(tokens.shape),
+        gain_grads[:, 0],
+        span(18, 20),
+        grads[20],
+        grads[21],
+        span(8, 10).T,
+        gain_grads[:, 1],
+        gate_grad,
+        up_grad,
+        down_grad.T,
+    )
+
+
+def fits(mesh):
+    return mesh.shape["fsdp"] == 4 and mesh.shape["ctx"] == 4 and mesh.shape["tp"] == 2
+
+
 def solution(mesh):
     placed = (
         P("fsdp", "ctx", None),
@@ -396,7 +1573,7 @@
         P("tp", ("fsdp", "ctx")),
     )
     return jax.shard_map(
-        body,
+        fast_body if fits(mesh) else body,
         mesh=mesh,
         in_specs=placed,
         out_specs=(

time: 1280 us -> 525 us (0.41)
  waiting for transfers between devices: 877 us -> 0 us
  Pallas kernels: 0 us -> 490 us
  matrix products: 179 us -> 0 us
  blocking collectives: 106 us -> 0 us
  other arithmetic: 58.5 us -> 4.4 us
  between operations: 19 us -> 3.11 us
    pallas_call x0 -> x2, Pallas kernels: none -> 490 us  [the longest x1 260 us: call_forward(): pl.pallas_call(forward_kernel, out_shape=(struct((units,) + block + (UNIT...]
    reduce_scatter x11 -> x0, waiting for transfers between devices: 478 us -> none  [the longest x1 87 us: grad_reduce(): lax.psum_scatter(gradients[8], ('fsdp', 'ctx'), scatter_dimension=1, tile...]
    all_gather x7 -> x0, waiting for transfers between devices: 207 us -> none  [the longest x1 60.5 us: weight_gather(): lax.all_gather(shards[5], ('fsdp', 'ctx'), axis=0, tiled=True)]
    psum x3 -> x0, waiting for transfers between devices: 185 us -> none  [head_sum(): return lax.psum(partial_rows.astype(jnp.bfloat16), 'tp').astype(jnp.float32)]
    dot_general x70 -> x0, matrix products: 179 us -> none  [the longest x8 23.5 us: block_scores(): jnp.einsum('qhgd,khd->hgqk', queries, key_block, preferred_element_type=j...]
    unnamed x2 -> x0, blocking collectives: 69.4 us -> none
    all_gather x4 -> x0, blocking collectives: 36.6 us -> none  [the longest x2 19.8 us: micro_step(): lax.all_gather(key_low, 'ctx', axis=0, tiled=True)]
    reduce_sum x10 -> x1, other arithmetic: 22.8 us -> 1.04 us  [fast_body(): jnp.sum((segments[:, None, :] < mine[:, :, None]).astype(jnp.int32), axis...]
  transfers between devices with their start and end apart: 21 -> 0, of which waited for: 18 -> 0; matrix products, arithmetic and copies ran while one was open for 15% -> 0% of each run, Pallas kernels for 0% -> 0%
where the time goes in v2:
time: 525 us; the launch traced here: 515 us
  Pallas kernels  490 us (93%)
  local copies, waits for them, and re-layouts  18.1 us (3%)
    pallas_call x1, Pallas kernels, call_forward(): pl.pallas_call(forward_kernel, out_shape=(struct((units,) + block + (UNIT...  260 us
    pallas_call x1, Pallas kernels, call_backward(): pl.pallas_call(backward_kernel, out_shape=(struct((ROWS, WIDE), BF16), st...  230 us

profile of v2, /device:TPU:0, one launch (start us, length us, event | category | flops | bytes accessed | tf_op | source)
XLA Modules:
  0.0 515.5 jit_solution(3387313947351090063)
XLA Ops:
  0.7 0.7 pad_maximum_fusion.11
  1.4 0.6 iota_add_fusion.high
  2.0 0.5 slice.147
  4.4 0.8 constant_dynamic-slice_fusion
  5.2 1.0 convert_reduce_fusion
  6.2 0.6 broadcast_in_dim.2.low
  7.0 0.6 pad.4.gains
  7.6 0.3 fusion.8
  7.9 0.9 copy.41.sine
  8.9 0.9 copy.40.cosine
  10.2 0.2 copy.48
  10.4 0.6 copy-done.7
  11.3 1.3 copy.50
  12.6 260.1 %forward.1 = (bf16[22,4,2,2,96,384]{5,4,3,2,1,0:T(8,128)(2,1)}, f32[8,1536]{1,0:T(8,128)}, bf16[1536,512]{1,0:T(8,128)(2,1)}, bf16[1536,512]{1,0:T(8,128)(2,1)},...) custom-call(bf16[22,96,384]{2,1,0:T(8,128)(2,1)} %bitcast.74, ...), custom_call_target="tpu_custom_call" | custom-call | tf_op jit(solution)/shard_map/forward/pallas_call | solution.py:815
  272.7 229.8 %backward.1 = (bf16[512,1536]{1,0:T(8,128)(2,1)}, f32[512,1536]{1,0:T(8,128)}, f32[22,96,384]{2,1,0:T(8,128)}, f32[96,128]{1,0:T(8,128)}) custom-call(bf16[22,4,2,2,96,384]{5,4,3,2,1,0:T(8,128)(2,1)} %get-tuple-element.30.w_all, f32[8,1536]{1,0:T(8,128)} %get-tuple-element.31.gain_rows, bf16[512,1536]{1,0:T(8,128)(2,1)} %bitcast.76, ...), custom_call_target="tpu_custom_call" | custom-call | tf_op jit(solution)/shard_map/backward/pallas_call | solution.py:1398
  502.5 1.6 slice_reduce_fusion
  504.0 1.7 slice_bitcast_fusion.19
  505.8 2.7 slice_bitcast_fusion
  508.5 0.7 pad_maximum_fusion.1
  509.2 0.7 maximum_bitcast_fusion
  510.3 1.9 copy-done.1
  512.2 1.1 copy.78
  513.4 0.2 copy-done
  513.6 1.7 copy.79
  (44 shorter events, 1.1 us)
Async XLA Ops:
  0.6 9.1 %copy-start.2 = (bf16[96,2048]{1,0:T(8,128)(2,1)S(1)}, bf16[96,2048]{1,0:T(8,128)(2,1)}, u32[]{:S(2)}) copy-start(bf16[96,2048]{1,0:T(8,128)(2,1)} %param.21) | copy-start | bytes 1179652
  7.8 2.0 copy-start.3
  7.9 2.1 copy-start.4
  10.1 0.9 copy-start.7
  10.1 0.9 copy-start.8
  10.2 1.0 copy-start.5
  10.2 1.0 copy-start.6
  510.1 2.1 copy-start.1
  510.2 5.0 copy-start.9
  510.3 5.0 copy-start.10
  510.3 5.0 copy-start.11
  510.3 3.3 copy-start

commit v3 on v1

--- a/solution.py
+++ b/solution.py
@@ -3,6 +3,8 @@
 import jax
 import jax.numpy as jnp
 from jax import lax
+from jax.experimental import pallas as pl
+from jax.experimental.pallas import tpu as pltpu
 from jax.sharding import PartitionSpec as P
 
 HD = 96
@@ -380,6 +382,1178 @@
     )
 
 
+MESH = pl.DeviceIdType.MESH
+UNIT = 384
+ROWS = 512
+SPAN = 256
+WIDE = 1536
+F32 = jnp.float32
+BF16 = jnp.bfloat16
+NT = (((1,), (1,)), ((), ()))
+TN = (((0,), (0,)), ((), ()))
+
+
+def dot_nn(a, b):
+    return jnp.dot(a, b, preferred_element_type=F32)
+
+
+def dot_nt(a, b):
+    return lax.dot_general(a, b, NT, preferred_element_type=F32)
+
+
+def dot_tn(a, b):
+    return lax.dot_general(a, b, TN, preferred_element_type=F32)
+
+
+class Place:
+    def __init__(self):
+        f, c, t = (lax.axis_index(axis) for axis in ("fsdp", "ctx", "tp"))
+        self.f, self.c, self.t = f, c, t
+        self.y, self.k = lax.div(c, 2), lax.rem(c, 2)
+        self.oy, self.ok = 1 - self.y, 1 - self.k
+        self.half = lax.div(f, 2)
+        self.inner = (f == 1) | (f == 2)
+        self.edge = (f == 0) | (f == 3)
+        self.near_f = f + 1 - 2 * lax.rem(f, 2)
+        self.mid_f = 2 - self.half
+        self.far_f = 3 - 3 * self.half
+        self.near = (self.near_f, c, t)
+        self.mid = (self.mid_f, c, t)
+        self.far = (self.far_f, c, t)
+        self.ypeer = (f, c + 2 - 4 * self.y, t)
+        self.sib = (f, c + 1 - 2 * self.k, t)
+        self.xpeer = (f, c, 1 - t)
+
+    def barrier(self):
+        sem = pltpu.get_barrier_semaphore()
+        others = [(lax.rem(self.f + step, 4), self.c, self.t) for step in (1, 2, 3)]
+        others += [self.ypeer, self.sib, self.xpeer]
+        for other in others:
+            pl.semaphore_signal(sem, inc=1, device_id=other, device_id_type=MESH)
+        pl.semaphore_wait(sem, len(others))
+
+
+def remote(src, dst, send, recv, device):
+    return pltpu.make_async_remote_copy(
+        src_ref=src,
+        dst_ref=dst,
+        send_sem=send,
+        recv_sem=recv,
+        device_id=device,
+        device_id_type=MESH,
+    )
+
+
+def lanes(rows, columns):
+    return lax.broadcasted_iota(jnp.int32, (rows, columns), 1)
+
+
+def unpack_heads(x):
+    lane = lanes(x.shape[0], 128)
+    one, two, three = x[:, :128], x[:, 128:256], x[:, 256:]
+    heads = (
+        one,
+        pltpu.roll(jnp.where(lane < 64, two, one), 32, 1),
+        pltpu.roll(jnp.where(lane < 32, three, two), 64, 1),
+        pltpu.roll(three, 96, 1),
+    )
+    return [jnp.where(lane < HD, head, 0.0) for head in heads]
+
+
+def pack_heads(heads):
+    lane = lanes(heads[0].shape[0], 128)
+    second = pltpu.roll(heads[1], 96, 1)
+    third = pltpu.roll(heads[2], 64, 1)
+    fourth = pltpu.roll(heads[3], 32, 1)
+    return jnp.concatenate(
+        [
+            jnp.where(lane < 96, heads[0], second),
+            jnp.where(lane < 64, second, third),
+            jnp.where(lane < 32, third, fourth),
+        ],
+        axis=1,
+    )
+
+
+def turn(x, cosine, sine):
+    lane = lax.rem(lanes(x.shape[0], UNIT), HD)
+    swapped = jnp.where(lane < HD // 2, pltpu.roll(x, UNIT - HD // 2, 1), pltpu.roll(x, HD // 2, 1))
+    return x * cosine + swapped * sine
+
+
+def transpose_into(dst, src):
+    @pl.loop(0, WIDE // 128)
+    def _(i):
+        at = pl.multiple_of(i * 128, 128)
+        dst[pl.ds(at, 128), :] = src[:, pl.ds(at, 128)].astype(F32).T.astype(BF16)
+
+
+def weight(buf, slot, lo, hi):
+    return buf[slot, :, :, :, :, lo:hi].reshape(WIDE, hi - lo)
+
+
+def allowed_keys(low_row, high_row):
+    row = lax.broadcasted_iota(jnp.int32, (4 * SPAN, SPAN), 0)
+    return (row >= low_row) & (row <= high_row)
+
+
+RING = 5
+WIDE_A = 256
+WIDE_B = 128
+
+
+class GatherA:
+    def __init__(self, me, buf, source, sems):
+        self.me, self.buf, self.source = me, buf, source
+        self.z_send, self.z_recv, self.y_send, self.y_recv, self.c_send, self.c_recv = sems
+
+    def z_copy(self, j, i):
+        me = self.me
+        dst = self.buf.at[j, me.f, me.y, me.k]
+        return remote(self.source.at[j], dst, self.z_send.at[j, i], self.z_recv.at[j], (me.near, me.mid)[i])
+
+    def hand_copy(self, j):
+        me = self.me
+        part = self.buf.at[j, pl.ds(2 - 2 * me.half, 2), me.y, me.k]
+        return remote(part, part, self.z_send.at[j, 2], self.z_recv.at[j], me.near)
+
+    def y_copy(self, j):
+        me = self.me
+        part = self.buf.at[j, :, me.y, me.k]
+        return remote(part, part, self.y_send.at[j], self.y_recv.at[j], me.ypeer)
+
+    def core_copy(self, j):
+        me = self.me
+        part = self.buf.at[j, :, :, me.k]
+        return remote(part, part, self.c_send.at[j], self.c_recv.at[j], me.sib)
+
+    def z_wait(self, j):
+        me = self.me
+        three = self.buf.at[j, pl.ds(0, 3), me.y, me.k]
+        remote(three, three, self.z_send.at[j, 0], self.z_recv.at[j], me.near).wait_recv()
+
+    def start(self, j):
+        for i in range(2):
+            self.z_copy(j, i).start()
+
+    def spread(self, j):
+        pass
+
+    def hand(self, j):
+        @pl.when(self.me.inner)
+        def _():
+            self.z_wait(j)
+            self.hand_copy(j).start()
+
+    def turn(self, j):
+        @pl.when(self.me.edge)
+        def _():
+            self.z_wait(j)
+
+        self.y_copy(j).start()
+
+    def core(self, j):
+        self.y_copy(j).wait_recv()
+        self.core_copy(j).start()
+
+    def done(self, j):
+        self.core_copy(j).wait_recv()
+
+    def sent(self, j):
+        for i in range(2):
+            self.z_copy(j, i).wait_send()
+
+        @pl.when(self.me.inner)
+        def _():
+            self.hand_copy(j).wait_send()
+
+        self.y_copy(j).wait_send()
+        self.core_copy(j).wait_send()
+
+
+class GatherB(GatherA):
+    def z_copy(self, j, i):
+        me = self.me
+        part = self.buf.at[j, me.f, :, me.k]
+        return remote(part, part, self.z_send.at[j, i], self.z_recv.at[j], (me.near, me.mid)[i])
+
+    def hand_copy(self, j):
+        me = self.me
+        part = self.buf.at[j, pl.ds(2 - 2 * me.half, 2), :, me.k]
+        return remote(part, part, self.z_send.at[j, 2], self.z_recv.at[j], me.near)
+
+    def y_copy(self, j):
+        me = self.me
+        dst = self.buf.at[j, me.f, me.y, me.k]
+        return remote(self.source.at[j], dst, self.y_send.at[j], self.y_recv.at[j], me.ypeer)
+
+    def z_wait(self, j):
+        me = self.me
+        three = self.buf.at[j, pl.ds(0, 3), :, me.k]
+        remote(three, three, self.z_send.at[j, 0], self.z_recv.at[j], me.near).wait_recv()
+
+    def start(self, j):
+        self.y_copy(j).start()
+
+    def spread(self, j):
+        self.y_copy(j).wait_recv()
+        for i in range(2):
+            self.z_copy(j, i).start()
+
+    def turn(self, j):
+        pass
+
+    def core(self, j):
+        @pl.when(self.me.edge)
+        def _():
+            self.z_wait(j)
+
+        self.core_copy(j).start()
+
+
+class ReduceA:
+    def __init__(self, me, r, other, mine, bufs, sems):
+        self.me, self.r, self.other, self.mine = me, r, other, mine
+        self.r1, self.r2, self.r3 = bufs
+        (
+            self.c_send,
+            self.c_recv,
+            self.y_send,
+            self.y_recv,
+            self.za_send,
+            self.za_recv,
+            self.zb_send,
+            self.zb_recv,
+        ) = sems
+        self.zed = self.r2
+
+    def core_copy(self):
+        return remote(self.other, self.r1, self.c_send.at[self.r], self.c_recv.at[self.r], self.me.sib)
+
+    def y_copy(self):
+        src = self.r1.at[:, self.me.oy]
+        return remote(src, self.r2, self.y_send.at[self.r], self.y_recv.at[self.r], self.me.ypeer)
+
+    def za_copy(self):
+        src = self.zed.at[pl.ds(1 - self.me.half, 3)]
+        dst = self.r3.at[pl.ds(0, 3)]
+        return remote(src, dst, self.za_send.at[self.r], self.za_recv.at[self.r], self.me.near)
+
+    def zb_copy(self, i):
+        me = self.me
+        owner, at, device = ((me.near_f, 0, me.near), (me.mid_f, 3, me.mid), (me.far_f, 1, me.far))[i]
+        recv = self.zb_recv.at[self.r, min(i, 1)]
+        return remote(self.zed.at[owner], self.r3.at[at], self.zb_send.at[self.r, i], recv, device)
+
+    def core(self):
+        self.core_copy().start()
+
+    def add_core(self):
+        self.core_copy().wait_recv()
+        self.r1[...] = self.r1[...] + self.mine[...]
+        self.core_copy().wait_send()
+
+    def z_first(self):
+        @pl.when(self.me.edge)
+        def _():
+            self.za_copy().start()
+
+    def z_second(self, before=None):
+        me = self.me
+
+        @pl.when(me.inner)
+        def _():
+            self.za_copy().wait_recv()
+            for owner in (me.mid_f, me.far_f):
+                self.zed[owner] = self.zed[owner] + self.r3[owner - (1 - me.half)]
+            if before is not None:
+                before()
+            for i in range(3):
+                self.zb_copy(i).start()
+
+    def z_total(self):
+        me = self.me
+        self.zb_copy(1).wait_recv()
+
+        @pl.when(me.edge)
+        def _():
+            self.zb_copy(0).wait_recv()
+
+        one = jnp.where(me.edge, 0, me.f - (1 - me.half))
+        two = jnp.where(me.edge, 1, 3)
+        return self.zed[me.f].astype(F32) + self.r3[one].astype(F32) + self.r3[two].astype(F32)
+
+    def z_sent(self):
+        @pl.when(self.me.edge)
+        def _():
+            self.za_copy().wait_send()
+
+        @pl.when(self.me.inner)
+        def _():
+            for i in range(3):
+                self.zb_copy(i).wait_send()
+
+    def y_start(self):
+        self.y_copy().start()
+
+    def y_add(self):
+        self.y_copy().wait_recv()
+        self.r2[...] = self.r2[...] + self.r1[:, self.me.y]
+        self.y_copy().wait_send()
+
+
+class ReduceB(ReduceA):
+    def __init__(self, *args):
+        super().__init__(*args)
+        self.zed = self.r1
+
+    def y_copy(self):
+        src = self.r1.at[self.me.f, self.me.oy]
+        return remote(src, self.r2, self.y_send.at[self.r], self.y_recv.at[self.r], self.me.ypeer)
+
+    def z_end(self):
+        self.r1[self.me.f] = self.z_total().astype(BF16)
+        self.z_sent()
+        self.y_copy().start()
+
+    def total(self):
+        self.y_copy().wait_recv()
+        out = self.r1[self.me.f, self.me.y].astype(F32) + self.r2[...].astype(F32)
+        self.y_copy().wait_send()
+        return out
+
+
+def layer_kernel(
+    packed_a,
+    packed_b,
+    gains,
+    tokens,
+    cot,
+    cosine,
+    sine,
+    low,
+    high,
+    output,
+    grad_tokens,
+    grads,
+    gain_grads,
+    wa,
+    wb,
+    fed,
+    gw,
+    gain_rows,
+    a_buf,
+    at,
+    bt,
+    et,
+    eb,
+    kvx,
+    qh,
+    kh,
+    vh,
+    lse,
+    ob,
+    x2,
+    acc,
+    out_acc,
+    wbuf,
+    part,
+    stage,
+    back,
+    ra1,
+    ra2,
+    ra3,
+    rb1,
+    rb2,
+    rb3,
+    gout,
+    xs,
+    xr,
+    doh,
+    heads,
+    dkh,
+    dvh,
+    rc,
+    ry,
+    dqb,
+    dkvb,
+    gacc,
+    gp,
+    g1,
+    g2,
+    g3,
+    gs,
+    ga_sems,
+    gb_sems,
+    gg_sems,
+    ra_sems,
+    rb_sems,
+    rg_sems,
+    c_cred,
+    y_cred,
+    z_cred,
+    x_cred,
+    x_send,
+    x_recv,
+    kv_send,
+    kv_recv,
+    g_sems,
+    load_sem,
+    w_sem,
+    stage_sem,
+    back_sem,
+    out_sem,
+):
+    me = Place()
+    f, y, k = me.f, me.y, me.k
+    units, depth = packed_a.shape[0], packed_a.shape[1]
+    groups = fed.shape[0]
+    scale = 1.0 / math.sqrt(HD)
+
+    def local(src, dst, i):
+        return pltpu.make_async_copy(src, dst, load_sem.at[i])
+
+    own = (
+        local(packed_a, wa.at[:, f, y, k], 0),
+        local(packed_b, wb.at[:, f, y, k], 1),
+        local(gains.at[0], gw.at[0, f, y, k], 2),
+    )
+    for copy in own:
+        copy.start()
+    local(cot, eb, 3).start()
+    me.barrier()
+
+    gather_a = GatherA(me, wa, packed_a, ga_sems)
+    gather_b = GatherB(me, wb, packed_b, gb_sems)
+    gather_g = GatherA(me, gw, gains, gg_sems)
+
+    def within(i, count, act):
+        if isinstance(i, int):
+            if 0 <= i < count:
+                act(i)
+        else:
+            pl.when((i >= 0) & (i < count))(lambda: act(i))
+
+    def ag(t):
+        def both(name):
+            def act(j):
+                getattr(gather_b, name)(j)
+                getattr(gather_a, name)(j)
+
+            return act
+
+        within(t + 5, units, both("start"))
+        within(t + 3, units, both("spread"))
+        within(t + 1, units, both("hand"))
+        within(t, units, both("turn"))
+        within(t - 1, units, both("core"))
+        within(t - 2, units, both("done"))
+
+    def load(u, slot, side):
+        at_b = side * UNIT + WIDE_A
+        return (
+            pltpu.make_async_copy(
+                wa.at[u], wbuf.at[slot, :, :, :, :, pl.ds(side * UNIT, WIDE_A)], w_sem.at[slot, side, 0]
+            ),
+            pltpu.make_async_copy(
+                wb.at[u], wbuf.at[slot, :, :, :, :, pl.ds(at_b, WIDE_B)], w_sem.at[slot, side, 1]
+            ),
+        )
+
+    def load_start(u, slot, side):
+        for copy in load(u, slot, side):
+            copy.start()
+
+    def load_wait(u, slot, side):
+        for copy in load(u, slot, side):
+            copy.wait()
+
+    def ring(r):
+        s = lax.rem(r, RING)
+        slot = lax.rem(lax.div(r, 2), 2)
+        start = lax.rem(r, 2) * UNIT
+        cols_a = pl.ds(pl.multiple_of(start, 128), WIDE_A)
+        cols_b = pl.ds(pl.multiple_of(start + WIDE_A, 128), WIDE_B)
+        one = ReduceA(
+            me,
+            r,
+            part.at[slot, :, :, me.ok, :, cols_a],
+            part.at[slot, :, :, k, :, cols_a],
+            (ra1.at[s], ra2.at[s], ra3.at[s]),
+            ra_sems,
+        )
+        two = ReduceB(
+            me,
+            r,
+            part.at[slot, :, :, me.ok, :, cols_b],
+            part.at[slot, :, :, k, :, cols_b],
+            (rb1.at[s], rb2.at[s], rb3.at[s]),
+            rb_sems,
+        )
+        return one, two
+
+    def credit(r, sem):
+        within(r - RING, units, lambda i: pl.semaphore_wait(sem, 1))
+
+    def give(r, sem, device):
+        def act(i):
+            pl.semaphore_signal(sem, inc=1, device_id=device, device_id_type=MESH)
+
+        within(r + RING, units, act)
+
+    def out_copy(i):
+        slot = lax.rem(i, 2)
+        return pltpu.make_async_copy(gout.at[slot], grads.at[i], out_sem.at[slot])
+
+    def rs(r):
+        def first(i):
+            credit(i, c_cred)
+            for unit in ring(i):
+                unit.core()
+
+        def second(i):
+            one, two = ring(i)
+            two.add_core()
+
+            @pl.when(me.edge)
+            def _():
+                credit(i, z_cred.at[0])
+
+            two.z_first()
+            one.add_core()
+            credit(i, y_cred)
+            one.y_start()
+
+        def third(i):
+            one, two = ring(i)
+
+            def take():
+                for j in range(3):
+                    credit(i, z_cred.at[j])
+
+            two.z_second(take)
+            one.y_add()
+            one.z_first()
+
+        def fourth(i):
+            one, two = ring(i)
+            one.z_second()
+            two.z_end()
+
+        def fifth(i):
+            one, two = ring(i)
+            slot = lax.rem(i, 2)
+            within(i - 2, units, lambda j: out_copy(j).wait())
+            gout[slot, :, 0:WIDE_A] = one.z_total()
+            one.z_sent()
+            gout[slot, :, WIDE_A:] = two.total()
+            out_copy(i).start()
+            give(i, c_cred, me.sib)
+            give(i, y_cred, me.ypeer)
+
+            @pl.when(me.edge)
+            def _():
+                give(i, z_cred.at[0], me.near)
+                give(i, z_cred.at[2], me.mid)
+
+            @pl.when(me.inner)
+            def _():
+                give(i, z_cred.at[0], me.near)
+                give(i, z_cred.at[1], me.mid)
+
+        within(r, units, first)
+        within(r - 1, units, second)
+        within(r - 2, units, third)
+        within(r - 3, units, fourth)
+        within(r - 4, units, fifth)
+
+    def put(pair, i, value):
+        columns = slice(i * 256, (i + 1) * 256)
+        part[lax.rem(pair, 2), :, :, :, :, columns] = value.astype(BF16).reshape(4, 2, 2, depth, 256)
+
+    def x_copy(e, r):
+        rows = pl.ds(pl.multiple_of(r * 128, 128), 128)
+        return remote(xs.at[rows], xr.at[rows], x_send.at[e, r], x_recv.at[e, r], me.xpeer)
+
+    def give_x():
+        pl.semaphore_signal(x_cred, inc=1, device_id=me.xpeer, device_id_type=MESH)
+
+    def take_x():
+        pl.semaphore_wait(x_cred, 1)
+
+    for copy in own:
+        copy.wait()
+    gather_g.start(0)
+    ag(-5)
+    ag(-4)
+    gather_g.hand(0)
+    gather_g.turn(0)
+    ag(-3)
+    local(cot, eb, 3).wait()
+    transpose_into(et, eb)
+    gather_g.core(0)
+    ag(-2)
+    gather_g.done(0)
+    gain_rows[...] = gw[0].reshape(WIDE, 128).astype(F32).T[:8, :]
+    ag(-1)
+
+    @pl.loop(0, ROWS // 64)
+    def _(i):
+        rows = pl.ds(pl.multiple_of(i * 64, 64), 64)
+        x = tokens[rows, :].astype(F32)
+        r = lax.rsqrt(jnp.mean(x * x, axis=-1, keepdims=True) + epsilon)
+        a_buf[rows, :] = (x * r * gain_rows[0:1, :]).astype(BF16)
+
+    ag(0)
+    transpose_into(at, a_buf)
+    ag(1)
+    ag(2)
+    load_start(0, 0, 0)
+    ag(3)
+    load_start(1, 0, 1)
+    load_wait(0, 0, 0)
+    for s in range(2):
+        rows = pl.ds(s * SPAN, SPAN)
+        key = turn(dot_nn(a_buf[rows, :], weight(wbuf, 0, 0, UNIT)), cosine[...], sine[...])
+        kvx[y, k, rows, 0:UNIT] = key.astype(BF16)
+    load_wait(1, 0, 1)
+    kvx[y, k, :, UNIT:] = dot_nn(a_buf[...], weight(wbuf, 0, UNIT, 2 * UNIT)).astype(BF16)
+
+    def kv_copy(i):
+        part_kv = kvx.at[y, k] if i == 0 else kvx.at[:, k]
+        return remote(part_kv, part_kv, kv_send.at[0, i], kv_recv.at[0, i], me.ypeer if i == 0 else me.sib)
+
+    kv_copy(0).start()
+    ag(4)
+    load_start(2, 1, 0)
+    ag(5)
+    load_start(3, 1, 1)
+    load_wait(2, 1, 0)
+    load_wait(3, 1, 1)
+    for side in range(2):
+        for s in range(2):
+            rows = pl.ds(s * SPAN, SPAN)
+            query = dot_nn(a_buf[rows, :], weight(wbuf, 1, side * UNIT, (side + 1) * UNIT))
+            query = turn(query, cosine[...], sine[...])
+            for i, head in enumerate(unpack_heads(query)):
+                qh[s * 8 + side * 4 + i] = head.astype(BF16)
+    kv_copy(0).wait_recv()
+    kv_copy(1).start()
+    ag(6)
+    load_start(4, 0, 0)
+    ag(7)
+    load_start(5, 0, 1)
+    kv_copy(1).wait_recv()
+
+    @pl.loop(0, 8)
+    def _(i):
+        s, c = lax.div(i, 4), lax.rem(i, 4)
+        block = kvx[lax.div(c, 2), lax.rem(c, 2), pl.ds(pl.multiple_of(s * SPAN, SPAN), SPAN), :]
+        rows = pl.ds(pl.multiple_of(c * SPAN, SPAN), SPAN)
+        for g, head in enumerate(unpack_heads(block[:, :UNIT].astype(F32))):
+            kh[s * 4 + g, rows, :] = head.astype(BF16)
+        for g, head in enumerate(unpack_heads(block[:, UNIT:].astype(F32))):
+            vh[s * 4 + g, rows, :] = head.astype(BF16)
+
+    def attend(i):
+        s, h = lax.div(i, 8), lax.rem(i, 8)
+        g = s * 4 + lax.div(h, 2)
+        scores = dot_nt(kh[g], qh[i]) * scale
+        scores = jnp.where(allowed_keys(low[s], high[...]), scores, negative)
+        top = jnp.max(scores, axis=0, keepdims=True)
+        p = jnp.exp(scores - top)
+        total = jnp.sum(p, axis=0, keepdims=True)
+        lse[i] = jnp.broadcast_to(top + jnp.log(total), (8, SPAN))
+        heads[h] = (dot_tn(vh[g], p.astype(BF16)) / total).T
+
+    for s in range(2):
+        pl.loop(8 * s, 8 * s + 8)(attend)
+        rows = slice(s * SPAN, (s + 1) * SPAN)
+        for side in range(2):
+            mixed = pack_heads([heads[side * 4 + i] for i in range(4)])
+            ob[rows, side * UNIT : (side + 1) * UNIT] = mixed.astype(BF16)
+        if s == 0:
+            load_wait(4, 0, 0)
+            load_wait(5, 0, 1)
+        xs[rows, :] = dot_nt(ob[rows, :], weight(wbuf, 0, 0, 2 * UNIT)).astype(BF16)
+        x_copy(0, 2 * s).start()
+        x_copy(0, 2 * s + 1).start()
+        ag(8 + s)
+
+    for s in range(2):
+        ag(10 + 2 * s)
+
+        @pl.loop(2 * s, 2 * s + 2)
+        def _(r):
+            x_copy(0, r).wait()
+            rows = pl.ds(pl.multiple_of(r * 128, 128), 128)
+            x = tokens[rows, :].astype(F32) + (xs[rows, :].astype(F32) + xr[rows, :].astype(F32))
+            x2[rows, :] = x
+            r2 = lax.rsqrt(jnp.mean(x * x, axis=-1, keepdims=True) + epsilon)
+            a_buf[rows, :] = (x * r2 * gain_rows[1:2, :]).astype(BF16)
+
+        ag(11 + 2 * s)
+    give_x()
+    transpose_into(bt, a_buf)
+    acc[...] = jnp.zeros_like(acc)
+    out_acc[...] = jnp.zeros_like(out_acc)
+
+    def stage_copy(n):
+        slot = lax.rem(n, 2)
+        return pltpu.make_async_copy(stage.at[slot], fed.at[n], stage_sem.at[slot])
+
+    def back_copy(n):
+        slot = lax.rem(n, 2)
+        return pltpu.make_async_copy(fed.at[n], back.at[slot], back_sem.at[slot])
+
+    def feed_grads(n, pair, ready):
+        slot = lax.rem(n, 2)
+        back_copy(n).wait()
+        put(pair, 0, dot_nn(bt[...], back[slot, 0]))
+        put(pair, 1, dot_nn(bt[...], back[slot, 1]))
+        put(pair, 2, dot_nn(et[...], back[slot, 2]))
+        if ready:
+            within(n + 1, groups, lambda i: back_copy(i).start())
+
+    @pl.loop(0, groups)
+    def _(n):
+        slot = lax.rem(n, 2)
+        ag(14 + n + jnp.maximum(n - 5, 0))
+
+        @pl.when((n == 5) | (n == 6))
+        def _():
+            ag(15 + n + jnp.maximum(n - 5, 0))
+
+        for side in range(2):
+            load_start(6 + 2 * n + side, slot, side)
+
+        @pl.when((n == 2) | (n == 4) | (n == 6))
+        def _():
+            pair = lax.div(n, 2) - 1
+            feed_grads(pair, pair, False)
+
+        @pl.when(n >= 2)
+        def _():
+            rs(n - 2)
+
+        @pl.when(n >= 1)
+        def _():
+            stage_copy(n - 1).wait()
+
+        @pl.when(lax.rem(n, 2) == 1)
+        def _():
+            back_copy(lax.div(n, 2)).start()
+
+        for side in range(2):
+            load_wait(6 + 2 * n + side, slot, side)
+        gate = dot_nn(a_buf[...], weight(wbuf, slot, 0, 256))
+        up = dot_nn(a_buf[...], weight(wbuf, slot, 256, 512))
+        sg = jax.nn.sigmoid(gate)
+        silu = gate * sg
+        stage[slot, 2] = (silu * up).astype(BF16)
+        dh = dot_nn(eb[...], weight(wbuf, slot, 512, 768))
+        stage[slot, 0] = (dh * up * sg * (1.0 + gate * (1.0 - sg))).astype(BF16)
+        stage[slot, 1] = (dh * silu).astype(BF16)
+        stage_copy(n).start()
+
+        @pl.loop(0, 4)
+        def _(i):
+            columns = pl.ds(pl.multiple_of(i * 4 * depth, 128), 4 * depth)
+
+            def rows_of(lo):
+                return wbuf[slot, i, :, :, :, lo : lo + 256].reshape(4 * depth, 256)
+
+            out_acc[:, columns] += dot_nt(stage[slot, 2], rows_of(512))
+            acc[:, columns] += dot_nt(stage[slot, 0], rows_of(0)) + dot_nt(stage[slot, 1], rows_of(256))
+
+    load_start(4, 0, 0)
+    load_start(5, 0, 1)
+    take_x()
+    for r in range(4):
+        rows = slice(r * 128, (r + 1) * 128)
+        xs[rows, :] = acc[rows, :].astype(BF16)
+        x_copy(1, r).start()
+    stage_copy(groups - 1).wait()
+
+    gacc[...] = jnp.zeros_like(gacc)
+
+    def norm_back(r):
+        x_copy(1, r).wait()
+        rows = pl.ds(pl.multiple_of(r * 128, 128), 128)
+        mine = xs[rows, :].astype(F32)
+        db = mine + xr[rows, :].astype(F32)
+        x = x2[rows, :]
+        r2 = lax.rsqrt(jnp.mean(x * x, axis=-1, keepdims=True) + epsilon)
+        n2 = x * r2
+        gacc[1:2, :] += jnp.sum(mine * n2, axis=0, keepdims=True)
+        scaled = db * gain_rows[1:2, :]
+        dx2 = eb[rows, :].astype(F32) + r2 * (scaled - n2 * jnp.mean(scaled * n2, axis=-1, keepdims=True))
+        acc[rows, :] = dx2
+        eb[rows, :] = dx2.astype(BF16)
+
+    feed_grads(3, 3, True)
+    rs(6)
+    rs(7)
+    pl.loop(0, 2)(norm_back)
+    feed_grads(4, 4, True)
+    rs(8)
+    rs(9)
+    pl.loop(2, 4)(norm_back)
+
+    give_x()
+    xs[...] = out_acc[...].astype(BF16)
+    take_x()
+    for r in range(4):
+        x_copy(2, r).start()
+
+    load_wait(4, 0, 0)
+    load_wait(5, 0, 1)
+    for s in range(2):
+        rows = slice(s * SPAN, (s + 1) * SPAN)
+        for side in range(2):
+            mixed = dot_nn(eb[rows, :], weight(wbuf, 0, side * UNIT, (side + 1) * UNIT)).astype(BF16)
+            for i, head in enumerate(unpack_heads(mixed.astype(F32))):
+                doh[s * 8 + side * 4 + i] = head.astype(BF16)
+    feed_grads(5, 5, True)
+    rs(10)
+    for side in range(2):
+        load_start(2 + side, 0, side)
+        load_start(side, 1, side)
+
+    def attend_back(i):
+        s, g = lax.div(i, 4), lax.rem(i, 4)
+        mask = allowed_keys(low[s], high[...])
+        dk = jnp.zeros((4 * SPAN, 128), F32)
+        dv = jnp.zeros((4 * SPAN, 128), F32)
+        for hh in range(2):
+            h = s * 8 + 2 * g + hh
+            scores = jnp.where(mask, dot_nt(kh[i], qh[h]) * scale, negative)
+            p = jnp.exp(scores - lse[h][0:1, :])
+            dp = dot_nt(vh[i], doh[h])
+            delta = jnp.sum(p * dp, axis=0, keepdims=True)
+            ds = (p * (dp - delta) * scale).astype(BF16)
+            dv += dot_nn(p.astype(BF16), doh[h])
+            dk += dot_nn(ds, qh[h])
+            heads[2 * g + hh] = dot_tn(kh[i], ds).T
+        dkh[g] = dk.astype(BF16)
+        dvh[g] = dv.astype(BF16)
+
+    def dkv_mine(s, core):
+        return kvx.at[:, core, pl.ds(pl.multiple_of(s * SPAN, SPAN), SPAN)]
+
+    def kv_core(s):
+        return remote(dkv_mine(s, me.ok), rc.at[s], kv_send.at[1, s], kv_recv.at[1, s], me.sib)
+
+    def kv_y(s):
+        return remote(rc.at[s, me.oy], ry.at[s], kv_send.at[2, s], kv_recv.at[2, s], me.ypeer)
+
+    def kv_add(s):
+        kv_core(s).wait_recv()
+        rc[s] = rc[s] + dkv_mine(s, k)[...]
+        kv_y(s).start()
+
+    kv_copy(0).wait_send()
+    kv_copy(1).wait_send()
+
+    @pl.loop(0, 2)
+    def _(s):
+        attend_back(4 * s)
+        attend_back(4 * s + 1)
+        rs(11 + 2 * s)
+        attend_back(4 * s + 2)
+        attend_back(4 * s + 3)
+        rows = pl.ds(pl.multiple_of(s * SPAN, SPAN), SPAN)
+        for c in range(4):
+            at_c = slice(c * SPAN, (c + 1) * SPAN)
+            for j, src in enumerate((dkh, dvh)):
+                kvx[c // 2, c % 2, rows, j * UNIT : (j + 1) * UNIT] = pack_heads(
+                    [src[g, at_c, :].astype(F32) for g in range(4)]
+                ).astype(BF16)
+        kv_core(s).start()
+        for side in range(2):
+            dq = turn(pack_heads([heads[side * 4 + j] for j in range(4)]), cosine[...], -sine[...])
+            dqb[rows, side * UNIT : (side + 1) * UNIT] = dq.astype(BF16)
+        feed_grads(6 + s, 6 + s, True)
+        rs(12 + 2 * s)
+        kv_add(s)
+
+    transpose_into(bt, eb)
+    for i in range(3):
+        put(8, i, dot_nn(bt[...], ob[:, i * 256 : (i + 1) * 256]))
+    rs(15)
+    rs(16)
+
+    for r in range(4):
+        rows = slice(r * 128, (r + 1) * 128)
+        x_copy(2, r).wait()
+        xs[rows, :] = (x2[rows, :] + (xs[rows, :].astype(F32) + xr[rows, :].astype(F32))).astype(BF16)
+    give_x()
+    local(xs, output, 0).start()
+    for i in range(3):
+        put(9, i, dot_nn(at[...], dqb[:, i * 256 : (i + 1) * 256]))
+    rs(17)
+    rs(18)
+    for side in range(2):
+        load_wait(2 + side, 0, side)
+        load_wait(side, 1, side)
+    for s in range(2):
+        rows = slice(s * SPAN, (s + 1) * SPAN)
+        kv_y(s).wait_recv()
+        total = rc[s, y].astype(F32) + ry[s].astype(F32)
+        dkvb[rows, :UNIT] = turn(total[:, :UNIT], cosine[...], -sine[...]).astype(BF16)
+        dkvb[rows, UNIT:] = total[:, UNIT:].astype(BF16)
+    for i in range(3):
+        put(10, i, dot_nn(at[...], dkvb[:, i * 256 : (i + 1) * 256]))
+    rs(19)
+    rs(20)
+    local(xs, output, 0).wait()
+    take_x()
+
+    def first_norm(rows):
+        x = tokens[rows, :].astype(F32)
+        r1 = lax.rsqrt(jnp.mean(x * x, axis=-1, keepdims=True) + epsilon)
+        return r1, x * r1
+
+    for s in range(2):
+        rows = slice(s * SPAN, (s + 1) * SPAN)
+        da = dot_nt(dqb[rows, :], weight(wbuf, 0, 0, 768)) + dot_nt(dkvb[rows, :], weight(wbuf, 1, 0, 768))
+        xs[rows, :] = da.astype(BF16)
+        x_copy(3, 2 * s).start()
+        x_copy(3, 2 * s + 1).start()
+    rs(21)
+
+    @pl.loop(0, 4)
+    def _(r):
+        rows = pl.ds(pl.multiple_of(r * 128, 128), 128)
+        gacc[0:1, :] += jnp.sum(xs[rows, :].astype(F32) * first_norm(rows)[1], axis=0, keepdims=True)
+
+    gain_columns = jnp.concatenate([gacc[...], jnp.zeros((120, WIDE), F32)], axis=0).T
+    gp[...] = gain_columns.astype(BF16).reshape(4, 2, 2, depth, 128)
+    gain = ReduceA(me, 0, gp.at[:, :, me.ok], gp.at[:, :, k], (g1, g2, g3), rg_sems)
+    gain.core()
+    rs(22)
+    gain.add_core()
+    gain.y_start()
+    rs(23)
+    gain.y_add()
+    gain.z_first()
+
+    @pl.loop(0, 4)
+    def _(r):
+        x_copy(3, r).wait()
+        rows = pl.ds(pl.multiple_of(r * 128, 128), 128)
+        da = xs[rows, :].astype(F32) + xr[rows, :].astype(F32)
+        r1, n1 = first_norm(rows)
+        scaled = da * gain_rows[0:1, :]
+        acc[rows, :] += r1 * (scaled - n1 * jnp.mean(scaled * n1, axis=-1, keepdims=True))
+
+    local(acc, grad_tokens, 0).start()
+    gain.z_second()
+    rs(24)
+    gs[0] = gain.z_total()
+    gain.z_sent()
+    pair_copy = remote(gs.at[0], gs.at[1], g_sems.at[0], g_sems.at[1], me.xpeer)
+    pair_copy.start()
+    rs(25)
+    pair_copy.wait()
+    gain_grads[...] = gs[0] + gs[1]
+    for s in range(2):
+        kv_core(s).wait_send()
+        kv_y(s).wait_send()
+    gather_g.sent(0)
+
+    @pl.loop(0, units)
+    def _(u):
+        gather_a.sent(u)
+        gather_b.sent(u)
+
+    out_copy(units - 2).wait()
+    out_copy(units - 1).wait()
+    local(acc, grad_tokens, 0).wait()
+
+
+def rope_inputs(row_count):
+    positions = lax.axis_index("ctx") * row_count + jnp.arange(row_count, dtype=jnp.int32)
+    cosine_table, sine_table = rope_tables(positions)
+    cosine = jnp.tile(cosine_table, (1, 2 * UNIT // HD))
+    sine = jnp.tile(jnp.concatenate([-sine_table, sine_table], axis=1), (1, UNIT // HD))
+    return positions, cosine, sine
+
+
+def pack_weights(w_query, w_key, w_value, w_out, w_gate, w_up, w_down):
+    depth = w_query.shape[0]
+    groups = w_gate.shape[1] // 256
+    fed = jnp.concatenate(
+        [part.reshape(depth, groups, 256) for part in (w_gate, w_up, w_down.T)], axis=2
+    ).reshape(depth, groups * 2 * UNIT)
+    flat = jnp.concatenate([w_key, w_value, w_query, w_out.T, fed], axis=1)
+    cut = jnp.transpose(flat.reshape(depth, flat.shape[1] // UNIT, UNIT), (1, 0, 2))
+    return cut[:, :, :WIDE_A], cut[:, :, WIDE_A:]
+
+
+def pack_gains(gain_attn, gain_mlp):
+    return jnp.pad(jnp.stack([gain_attn, gain_mlp], axis=1), ((0, 0), (0, 126)))[None]
+
+
+def call_layer(packed_a, packed_b, gains, tokens, cot, cosine, sine, low, high):
+    units, depth = packed_a.shape[0], packed_a.shape[1]
+    groups = (units - 6) // 2
+    struct = jax.ShapeDtypeStruct
+    vmem = pltpu.VMEM
+    any_spec = pl.BlockSpec(memory_space=pl.ANY)
+    vmem_spec = pl.BlockSpec(memory_space=pltpu.VMEM)
+    block = (4, 2, 2, depth)
+    dma = pltpu.SemaphoreType.DMA
+    regular = pltpu.SemaphoreType.REGULAR
+
+    def gather_sems(count):
+        return (dma((count, 3)),) + tuple(dma((count,)) for _ in range(5))
+
+    def reduce_sems(count):
+        return tuple(dma((count,)) for _ in range(6)) + (dma((count, 3)), dma((count, 2)))
+
+    return pl.pallas_call(
+        layer_kernel,
+        out_shape=(
+            struct((ROWS, WIDE), BF16),
+            struct((ROWS, WIDE), F32),
+            struct((units, depth, UNIT), F32),
+            struct((depth, 128), F32),
+            struct((units,) + block + (WIDE_A,), BF16),
+            struct((units,) + block + (WIDE_B,), BF16),
+            struct((groups, 3, ROWS, 256), BF16),
+        ),
+        in_specs=[any_spec] * 3 + [vmem_spec, any_spec] + [vmem_spec] * 4,
+        out_specs=(any_spec,) * 3 + (vmem_spec,) + (any_spec,) * 3,
+        scratch_shapes=[
+            vmem((1,) + block + (128,), BF16),
+            vmem((8, WIDE), F32),
+            vmem((ROWS, WIDE), BF16),
+            vmem((WIDE, ROWS), BF16),
+            vmem((WIDE, ROWS), BF16),
+            vmem((WIDE, ROWS), BF16),
+            vmem((ROWS, WIDE), BF16),
+            vmem((2, 2, ROWS, 2 * UNIT), BF16),
+            vmem((16, SPAN, 128), BF16),
+            vmem((8, 4 * SPAN, 128), BF16),
+            vmem((8, 4 * SPAN, 128), BF16),
+            vmem((16, 8, SPAN), F32),
+            vmem((ROWS, 2 * UNIT), BF16),
+            vmem((ROWS, WIDE), F32),
+            vmem((ROWS, WIDE), F32),
+            vmem((ROWS, WIDE), F32),
+            vmem((2,) + block + (2 * UNIT,), BF16),
+            vmem((2,) + block + (2 * UNIT,), BF16),
+            vmem((2, 3, ROWS, 256), BF16),
+            vmem((2, 3, ROWS, 256), BF16),
+            vmem((RING, 4, 2, depth, WIDE_A), BF16),
+            vmem((RING, 4, depth, WIDE_A), BF16),
+            vmem((RING, 4, depth, WIDE_A), BF16),
+            vmem((RING, 4, 2, depth, WIDE_B), BF16),
+            vmem((RING, depth, WIDE_B), BF16),
+            vmem((RING, 4, 2, depth, WIDE_B), BF16),
+            vmem((2, depth, UNIT), F32),
+            vmem((ROWS, WIDE), BF16),
+            vmem((ROWS, WIDE), BF16),
+            vmem((16, SPAN, 128), BF16),
+            vmem((8, SPAN, 128), F32),
+            vmem((4, 4 * SPAN, 128), BF16),
+            vmem((4, 4 * SPAN, 128), BF16),
+            vmem((2, 2, SPAN, 2 * UNIT), BF16),
+            vmem((2, SPAN, 2 * UNIT), BF16),
+            vmem((ROWS, 2 * UNIT), BF16),
+            vmem((ROWS, 2 * UNIT), BF16),
+            vmem((8, WIDE), F32),
+            vmem(block + (128,), BF16),
+            vmem((4, 2, depth, 128), BF16),
+            vmem((4, depth, 128), BF16),
+            vmem((4, depth, 128), BF16),
+            vmem((2, depth, 128), F32),
+            gather_sems(units),
+            gather_sems(units),
+            gather_sems(1),
+            reduce_sems(units),
+            reduce_sems(units),
+            reduce_sems(1),
+            regular,
+            regular,
+            regular((3,)),
+            regular,
+            dma((4, 4)),
+            dma((4, 4)),
+            dma((3, 2)),
+            dma((3, 2)),
+            dma((2,)),
+            dma((4,)),
+            dma((2, 2, 2)),
+            dma((2,)),
+            dma((2,)),
+            dma((2,)),
+        ],
+        compiler_params=pltpu.CompilerParams(
+            collective_id=1, has_side_effects=True, vmem_limit_bytes=64 << 20
+        ),
+        name="layer",
+    )(packed_a, packed_b, gains, tokens, cot, cosine, sine, low, high)
+
+
+def fast_body(
+    tokens,
+    segments,
+    cotangent,
+    gain_attn,
+    w_query,
+    w_key,
+    w_value,
+    w_out,
+    gain_mlp,
+    w_gate,
+    w_up,
+    w_down,
+):
+    positions, cosine, sine = rope_inputs(SPAN)
+    mine = lax.dynamic_slice_in_dim(segments, positions[0], SPAN, 1)
+    low = jnp.sum((segments[:, None, :] < mine[:, :, None]).astype(jnp.int32), axis=-1)[:, None, :]
+    high = positions[None, :]
+    packed_a, packed_b = pack_weights(w_query, w_key, w_value, w_out, w_gate, w_up, w_down)
+    output, grad_tokens, grads, gain_grads = call_layer(
+        packed_a,
+        packed_b,
+        pack_gains(gain_attn, gain_mlp),
+        tokens.reshape(ROWS, WIDE),
+        cotangent.reshape(ROWS, WIDE),
+        cosine,
+        sine,
+        low,
+        high,
+    )[:4]
+
+    def span(lo, hi):
+        return jnp.concatenate([grads[i] for i in range(lo, hi)], axis=1)
+
+    fed = [span(2 * i, 2 * i + 2) for i in range(8)]
+    gate_grad, up_grad, down_grad = (
+        jnp.concatenate([group[:, i * 256 : (i + 1) * 256] for group in fed], axis=1) for i in range(3)
+    )
+    return (
+        output.reshape(tokens.shape),
+        grad_tokens.reshape(tokens.shape),
+        gain_grads[:, 0],
+        span(18, 20),
+        grads[20],
+        grads[21],
+        span(16, 18).T,
+        gain_grads[:, 1],
+        gate_grad,
+        up_grad,
+        down_grad.T,
+    )
+
+
+def fits(mesh):
+    return mesh.shape["fsdp"] == 4 and mesh.shape["ctx"] == 4 and mesh.shape["tp"] == 2
+
+
 def solution(mesh):
     placed = (
         P("fsdp", "ctx", None),
@@ -396,7 +1570,7 @@
         P("tp", ("fsdp", "ctx")),
     )
     return jax.shard_map(
-        body,
+        fast_body if fits(mesh) else body,
         mesh=mesh,
         in_specs=placed,
         out_specs=(

time: 1280 us -> 451 us (0.35)
  waiting for transfers between devices: 877 us -> 0 us
  Pallas kernels: 0 us -> 416 us
  matrix products: 179 us -> 0 us
  blocking collectives: 106 us -> 0 us
  other arithmetic: 58.5 us -> 4.4 us
  between operations: 19 us -> 3.32 us
    reduce_scatter x11 -> x0, waiting for transfers between devices: 478 us -> none  [the longest x1 87 us: grad_reduce(): lax.psum_scatter(gradients[8], ('fsdp', 'ctx'), scatter_dimension=1, tile...]
    pallas_call x0 -> x1, Pallas kernels: none -> 416 us  [call_layer(): pl.pallas_call(layer_kernel, out_shape=(struct((ROWS, WIDE), BF16), struc...]
    all_gather x7 -> x0, waiting for transfers between devices: 207 us -> none  [the longest x1 60.5 us: weight_gather(): lax.all_gather(shards[5], ('fsdp', 'ctx'), axis=0, tiled=True)]
    psum x3 -> x0, waiting for transfers between devices: 185 us -> none  [head_sum(): return lax.psum(partial_rows.astype(jnp.bfloat16), 'tp').astype(jnp.float32)]
    dot_general x70 -> x0, matrix products: 179 us -> none  [the longest x8 23.5 us: block_scores(): jnp.einsum('qhgd,khd->hgqk', queries, key_block, preferred_element_type=j...]
    unnamed x2 -> x0, blocking collectives: 69.4 us -> none
    all_gather x4 -> x0, blocking collectives: 36.6 us -> none  [the longest x2 19.8 us: micro_step(): lax.all_gather(key_low, 'ctx', axis=0, tiled=True)]
    reduce_sum x10 -> x1, other arithmetic: 22.8 us -> 1.04 us  [fast_body(): jnp.sum((segments[:, None, :] < mine[:, :, None]).astype(jnp.int32), axis...]
  transfers between devices with their start and end apart: 21 -> 0, of which waited for: 18 -> 0; matrix products, arithmetic and copies ran while one was open for 15% -> 0% of each run, Pallas kernels for 0% -> 0%
where the time goes in v3:
time: 451 us; the launch traced here: 442 us
  Pallas kernels  416 us (92%)
  local copies, waits for them, and re-layouts  19 us (4%)
    pallas_call x1, Pallas kernels, call_layer(): pl.pallas_call(layer_kernel, out_shape=(struct((ROWS, WIDE), BF16), struc...  416 us

profile of v3, /device:TPU:0, one launch (start us, length us, event | category | flops | bytes accessed | tf_op | source)
XLA Modules:
  0.0 442.4 jit_solution(2235281603395827505)
XLA Ops:
  0.7 0.7 pad_maximum_fusion.11
  1.4 0.6 iota_add_fusion.high
  2.0 0.5 slice.155
  4.4 0.8 constant_dynamic-slice_fusion
  5.2 1.0 convert_reduce_fusion
  6.2 0.6 broadcast_in_dim.5.low
  7.0 0.6 pad_bitcast_fusion.gains
  7.6 0.3 fusion.8
  7.9 0.9 copy.37.sine
  8.9 0.9 copy.36.cosine
  10.2 0.2 copy.42
  10.4 0.6 copy-done.7
  11.5 0.9 slice.205.packed_b
  12.4 1.1 slice.204.packed_a
  13.5 415.7 %layer.1 = (bf16[512,1536]{1,0:T(8,128)(2,1)}, f32[512,1536]{1,0:T(8,128)}, f32[22,96,384]{2,1,0:T(8,128)}, f32[96,128]{1,0:T(8,128)}, bf16[22,4,2,2,96,256]{5,4...) custom-call(bf16[22,96,256]{2,1,0:T(8,128)(2,1)} %slice.204.packed_a, ...), custom_call_target="tpu_custom_call" | custom-call | tf_op jit(solution)/shard_map/layer/pallas_call | solution.py:1415
  429.2 1.6 slice_reduce_fusion
  430.7 1.7 slice_bitcast_fusion.19
  432.5 2.7 slice_bitcast_fusion
  435.2 0.7 pad_maximum_fusion.1
  435.9 0.7 maximum_bitcast_fusion
  437.0 1.9 copy-done.1
  438.9 1.1 copy.72
  440.1 0.2 copy-done
  440.3 1.7 copy.73
  (45 shorter events, 1.2 us)
Async XLA Ops:
  0.6 9.1 %copy-start.2 = (bf16[96,2048]{1,0:T(8,128)(2,1)S(1)}, bf16[96,2048]{1,0:T(8,128)(2,1)}, u32[]{:S(2)}) copy-start(bf16[96,2048]{1,0:T(8,128)(2,1)} %param.21) | copy-start | bytes 1179652
  7.8 2.0 copy-start.3
  7.9 2.1 copy-start.4
  10.1 0.9 copy-start.7
  10.1 0.9 copy-start.8
  10.2 1.0 copy-start.5
  10.2 1.0 copy-start.6
  436.8 2.1 copy-start.1
  436.9 5.0 %copy-start.9 = (f32[96,2048]{1,0:T(8,128)}, f32[96,2048]{1,0:T(8,128)S(1)}, u32[]{:S(2)}) copy-start(f32[96,2048]{1,0:T(8,128)S(1)} %get-tuple-element.43) | copy-start | bytes 2359300
  437.0 5.0 %copy-start.10 = (f32[96,2048]{1,0:T(8,128)}, f32[96,2048]{1,0:T(8,128)S(1)}, u32[]{:S(2)}) copy-start(f32[96,2048]{1,0:T(8,128)S(1)} %get-tuple-element.92) | copy-start | bytes 2359300
  437.0 5.0 %copy-start.11 = (f32[96,2048]{1,0:T(8,128)}, f32[96,2048]{1,0:T(8,128)S(1)}, u32[]{:S(2)}) copy-start(f32[96,2048]{1,0:T(8,128)S(1)} %get-tuple-element.91) | copy-start | bytes 2359300
  437.0 3.3 copy-start
